TPU v7x, 128 devices: a whole 4x4x4 slice. The times are simulated.
128 devices in a mesh: layer: 4 (over x_hi, core), prow: 2 (over x_lo), pcol: 16 (over z, y).
Axes of the slice: x: 4 (x_hi: 2, x_lo: 2; x = x_hi * 2 + x_lo), y: 4, z: 4, core: 2. Of those that a mesh axis runs over, the one named last changes fastest.
Arguments:
- sub_rhs: float32 [4, 2, 16, 5, 32, 128], P('layer', 'prow', 'pcol'), may hold values from -6 to 6
- sub_lower_inverse: float32 [4, 2, 16, 5, 128, 128], P('layer', 'prow', 'pcol')
- sub_upper_inverse: float32 [4, 2, 16, 5, 128, 128], P('layer', 'prow', 'pcol')
- sub_lower: bfloat16 [4, 2, 16, 5, 16, 128, 128], P('layer', 'prow', 'pcol'), may hold values from -0.078125 to 0.078125
- sub_upper: bfloat16 [4, 2, 16, 5, 16, 128, 128], P('layer', 'prow', 'pcol'), may hold values from -0.078125 to 0.078125
- sub_source: int32 [4, 2, 16, 5, 16], P('layer', 'prow', 'pcol'), may hold values from 0 to 1
- sub_target: int32 [4, 2, 16, 5, 16], P('layer', 'prow', 'pcol'), may hold values from 0 to 31
- top_rhs: float32 [2, 16, 3, 32, 128], P('prow', 'pcol'), may hold values from -6 to 6
- top_lower_inverse: float32 [2, 16, 3, 128, 128], P('prow', 'pcol')
- top_upper_inverse: float32 [2, 16, 3, 128, 128], P('prow', 'pcol')
- top_lower: bfloat16 [2, 16, 2, 16, 128, 128], P('prow', 'pcol'), may hold values from -0.078125 to 0.078125
- top_upper: bfloat16 [2, 16, 2, 16, 128, 128], P('prow', 'pcol'), may hold values from -0.078125 to 0.078125
- top_source: int32 [2, 16, 2, 16], P('prow', 'pcol'), may hold values from 0 to 1
- top_target: int32 [2, 16, 2, 16], P('prow', 'pcol'), may hold values from 0 to 31, as said below
Outputs:
- sub_solution: float32 [4, 2, 16, 5, 32, 128], P('layer', 'prow', 'pcol')
- top_solution: float32 [2, 16, 3, 32, 128], P('prow', 'pcol')
Inputs may be any that keep to these rules, and one draw needn't show every extreme that they name: `top_target`: at the last ancestor level of slots every code is below 16.
All inputs are finite; a program needn't handle non-finite values.
Results may differ from a plain program's by a relative error of at most 0.015.
Values may be sent and summed in bfloat16 or wider, within the bound.
A program may use at most 64 MiB of HBM per device.

v0:
```python
import jax
import jax.numpy as jnp
from jax import lax
from jax.sharding import PartitionSpec as P


def apply_inverse(remainder, inverse):
    return jnp.dot(
        remainder, inverse, precision=lax.Precision.HIGHEST, preferred_element_type=jnp.float32
    )


def lower_terms(values, blocks, source, target):
    col_count = lax.axis_size("pcol")
    gathered = lax.all_gather(values.astype(jnp.bfloat16)[None], "prow", axis=0, tiled=True)
    picked = jnp.take(gathered, source, axis=0)
    products = jnp.einsum("kqw,kwv->kqv", picked, blocks, preferred_element_type=jnp.float32)
    column_code = target % col_count * 2 + target // col_count
    target_hot = (
        column_code[None, :] == jnp.arange(2 * col_count, dtype=jnp.int32)[:, None]
    ).astype(jnp.float32)
    shares = jnp.einsum("tk,kqv->qtv", target_hot, products, precision=lax.Precision.HIGHEST)
    return shares.reshape((products.shape[1], col_count, 2, products.shape[2]))


def upper_terms(ahead_values, blocks, source, target):
    row_count = lax.axis_size("prow")
    picked = jnp.take(ahead_values, target, axis=0)
    products = jnp.einsum("kqw,kwv->kqv", picked, blocks, preferred_element_type=jnp.float32)
    source_hot = (source[None, :] == jnp.arange(row_count, dtype=jnp.int32)[:, None]).astype(
        jnp.float32
    )
    shares = jnp.einsum("jk,kqv->qjv", source_hot, products, precision=lax.Precision.HIGHEST)
    flat_shares = shares.reshape((products.shape[1], row_count * products.shape[2]))
    return lax.psum_scatter(
        flat_shares.astype(jnp.bfloat16), "prow", scatter_dimension=1, tiled=True
    ).astype(jnp.float32)


def column_reduce(shares):
    side_count = shares.shape[0]
    block_width = shares.shape[3]
    flat_shares = shares.reshape((side_count, shares.shape[1] * 2 * block_width))
    reduced = lax.psum_scatter(flat_shares, "pcol", scatter_dimension=1, tiled=True)
    return reduced.reshape((side_count, 2, block_width))


def gather_solution(values):
    return lax.all_gather(values.astype(jnp.bfloat16)[None], "pcol", axis=0, tiled=True)


def local(
    sub_rhs,
    sub_lower_inverse,
    sub_upper_inverse,
    sub_lower,
    sub_upper,
    sub_source,
    sub_target,
    top_rhs,
    top_lower_inverse,
    top_upper_inverse,
    top_lower,
    top_upper,
    top_source,
    top_target,
):
    sub_levels = sub_rhs.shape[3]
    top_levels = top_rhs.shape[2]
    all_levels = sub_levels + top_levels
    side_count = sub_rhs.shape[4]
    block_width = sub_rhs.shape[5]
    col_count = lax.axis_size("pcol")
    rhs_list = [sub_rhs[0, 0, 0, height] for height in range(sub_levels)] + [
        top_rhs[0, 0, height] for height in range(top_levels)
    ]
    lower_inv = [sub_lower_inverse[0, 0, 0, height] for height in range(sub_levels)] + [
        top_lower_inverse[0, 0, height] for height in range(top_levels)
    ]
    upper_inv = [sub_upper_inverse[0, 0, 0, height] for height in range(sub_levels)] + [
        top_upper_inverse[0, 0, height] for height in range(top_levels)
    ]
    lower_blocks = [sub_lower[0, 0, 0, height] for height in range(sub_levels)] + [
        top_lower[0, 0, height] for height in range(top_levels - 1)
    ]
    upper_blocks = [sub_upper[0, 0, 0, height] for height in range(sub_levels)] + [
        top_upper[0, 0, height] for height in range(top_levels - 1)
    ]
    sources = [sub_source[0, 0, 0, height] for height in range(sub_levels)] + [
        top_source[0, 0, height] for height in range(top_levels - 1)
    ]
    targets = [sub_target[0, 0, 0, height] for height in range(sub_levels)] + [
        top_target[0, 0, height] for height in range(top_levels - 1)
    ]
    nothing = jnp.zeros((side_count, block_width), jnp.float32)
    solved = []
    arrived = [nothing] * all_levels
    ancestral = [nothing, nothing]
    for height in range(all_levels):
        if height == sub_levels:
            first_sum, second_sum = (
                lax.psum(ancestral[0].astype(jnp.bfloat16), "layer").astype(jnp.float32),
                lax.psum(ancestral[1].astype(jnp.bfloat16), "layer").astype(jnp.float32),
            )
            arrived[height] = first_sum
            arrived[height + 1] = second_sum
        values = apply_inverse(rhs_list[height] - arrived[height], lower_inv[height])
        solved.append(values)
        if height < all_levels - 1:
            reduced = column_reduce(
                lower_terms(values, lower_blocks[height], sources[height], targets[height])
            )
            for offset in range(2):
                destination = height + 1 + offset
                if height < sub_levels and destination >= sub_levels:
                    ancestral[destination - sub_levels] = (
                        ancestral[destination - sub_levels] + reduced[:, offset]
                    )
                elif destination < all_levels:
                    arrived[destination] = arrived[destination] + reduced[:, offset]
    finished = [None] * all_levels
    shared = [None] * all_levels
    for height in reversed(range(all_levels)):
        remainder = solved[height]
        if height < all_levels - 1:
            if height + 2 < all_levels:
                farther = shared[height + 2]
            else:
                farther = jnp.zeros((col_count, side_count, block_width), jnp.bfloat16)
            ahead_values = jnp.concatenate([shared[height + 1], farther], axis=0)
            remainder = remainder - upper_terms(
                ahead_values, upper_blocks[height], sources[height], targets[height]
            )
        values = apply_inverse(remainder, upper_inv[height])
        finished[height] = values
        if height > 0:
            shared[height] = gather_solution(values)
    sub_solution = jnp.stack(finished[:sub_levels])[None, None, None]
    top_solution = jnp.stack(finished[sub_levels:])[None, None]
    return (sub_solution, top_solution)


def solution(mesh):
    in_specs = (
        P("layer", "prow", "pcol", None, None, None),
        P("layer", "prow", "pcol", None, None, None),
        P("layer", "prow", "pcol", None, None, None),
        P("layer", "prow", "pcol", None, None, None, None),
        P("layer", "prow", "pcol", None, None, None, None),
        P("layer", "prow", "pcol", None, None),
        P("layer", "prow", "pcol", None, None),
        P("prow", "pcol", None, None, None),
        P("prow", "pcol", None, None, None),
        P("prow", "pcol", None, None, None),
        P("prow", "pcol", None, None, None, None),
        P("prow", "pcol", None, None, None, None),
        P("prow", "pcol", None, None),
        P("prow", "pcol", None, None),
    )
    out_specs = (P("layer", "prow", "pcol", None, None, None), P("prow", "pcol", None, None, None))
    return jax.shard_map(local, mesh=mesh, in_specs=in_specs, out_specs=out_specs, check_vma=False)
```

profile of v0, /device:TPU:0, one launch (start us, length us, event | category | flops | bytes accessed | tf_op | source)
XLA Modules:
  0.0 879.8 jit_solution(124145035558974094)
XLA Ops:
  7.2 1.8 fusion.274
  9.0 4.4 all-gather
  15.4 1.3 fusion.34
  17.4 1.1 copy.121
  18.5 75.0 %reduce-scatter.29.cloned.1.call-done = f32[32,256]{1,0:T(8,128)} async-done(((f32[32,4096]{1,0:T(8,128)}), f32[32,256]{1,0:T(8,128)}) %reduce-scatter.29.cloned.1.call-update) | async-done | bytes 32784 | tf_op jit(solution)/shard_map/reduce_scatter | solution.py:44
  94.6 4.4 all-gather.1
  100.4 1.1 copy.120
  101.6 71.8 %reduce-scatter.31.cloned.1.call-done = f32[32,256]{1,0:T(8,128)} async-done(((f32[32,4096]{1,0:T(8,128)}), f32[32,256]{1,0:T(8,128)}) %reduce-scatter.31.cloned.1.call-update) | async-done | bytes 32784 | tf_op jit(solution)/shard_map/reduce_scatter | solution.py:44
  175.0 4.4 all-gather.2
  180.8 1.1 copy.119
  181.9 71.7 %reduce-scatter.33.cloned.1.call-done = f32[32,256]{1,0:T(8,128)} async-done(((f32[32,4096]{1,0:T(8,128)}), f32[32,256]{1,0:T(8,128)}) %reduce-scatter.33.cloned.1.call-update) | async-done | bytes 32784 | tf_op jit(solution)/shard_map/reduce_scatter | solution.py:44
  255.2 4.4 all-gather.3
  261.1 1.1 copy.118
  262.3 71.8 %reduce-scatter.35.cloned.1.call-done = f32[32,256]{1,0:T(8,128)} async-done(((f32[32,4096]{1,0:T(8,128)}), f32[32,256]{1,0:T(8,128)}) %reduce-scatter.35.cloned.1.call-update) | async-done | bytes 32784 | tf_op jit(solution)/shard_map/reduce_scatter | solution.py:44
  335.6 4.4 all-gather.4
  341.4 1.1 copy.117
  342.7 71.7 %reduce-scatter.37.cloned.1.call-done = f32[32,256]{1,0:T(8,128)} async-done(((f32[32,4096]{1,0:T(8,128)}), f32[32,256]{1,0:T(8,128)}) %reduce-scatter.37.cloned.1.call-update) | async-done | bytes 32784 | tf_op jit(solution)/shard_map/reduce_scatter | solution.py:44
  415.2 13.8 %all-reduce.1 = (bf16[32,128]{1,0:T(8,128)(2,1)S(1)}, bf16[32,128]{1,0:T(8,128)(2,1)S(1)}) all-reduce(bf16[32,128]{1,0:T(8,128)(2,1)S(1)} %get-tuple-element.97, bf16[32,128]{1,0:T(8,128)(2,1)S(1)} %get-tuple-element.96), channel_id=1, replica_groups=mesh['layer'=4,'prow'=2,'pcol'=16] {'layer'}, use_global_device_ids=true, to_apply=%region_5.7 | all-reduce | flops 8192 | bytes 32768 | tf_op jit(solution)/shard_map/psum | solution.py:102
  429.1 1.5 fusion.279
  430.6 4.4 all-gather.5
  436.4 1.1 copy.116
  437.6 71.2 %reduce-scatter.39.cloned.1.call-done = f32[32,256]{1,0:T(8,128)} async-done(((f32[32,4096]{1,0:T(8,128)}), f32[32,256]{1,0:T(8,128)}) %reduce-scatter.39.cloned.1.call-update) | async-done | bytes 32784 | tf_op jit(solution)/shard_map/reduce_scatter | solution.py:44
  510.3 4.4 all-gather.6
  519.7 69.4 %reduce-scatter.41.cloned.1.call-done = f32[32,256]{1,0:T(8,128)} async-done(((f32[32,4096]{1,0:T(8,128)}), f32[32,256]{1,0:T(8,128)}) %reduce-scatter.41.cloned.1.call-update) | async-done | bytes 32784 | tf_op jit(solution)/shard_map/reduce_scatter | solution.py:44
  590.8 23.0 %all-gather.7 = bf16[512,128]{1,0:T(8,128)(2,1)S(1)} all-gather(bf16[32,128]{1,0:T(8,128)(2,1)S(1)} %get-tuple-element.82), channel_id=9, replica_groups=mesh['layer'=4,'prow'=2,'pcol'=16] {'pcol'}, dimensions={0}, use_global_device_ids=true | all-gather | bytes 139264 | tf_op jit(solution)/shard_map/all_gather | solution.py:49
  614.4 1.5 fusion.20
  617.1 1.2 pad_clamp_fusion.5
  618.4 9.8 %reduce-scatter.43.cloned.1.call-done = bf16[128,32]{1,0:T(8,128)(2,1)} async-done(((bf16[256,32]{1,0:T(8,128)(2,1)}), bf16[128,32]{1,0:T(8,128)(2,1)}) %reduce-scatter.43.cloned.1.call-update) | async-done | bytes 8208
  629.0 1.5 fusion.282
  630.5 23.8 %all-gather.8 = bf16[512,128]{1,0:T(8,128)(2,1)S(1)} all-gather(bf16[32,128]{1,0:T(8,128)(2,1)S(1)} %get-tuple-element.84), channel_id=10, replica_groups=mesh['layer'=4,'prow'=2,'pcol'=16] {'pcol'}, dimensions={0}, use_global_device_ids=true | all-gather | bytes 139264 | tf_op jit(solution)/shard_map/all_gather | solution.py:49
  655.1 1.3 fusion.18
  659.1 10.7 %reduce-scatter.45.cloned.1.call-done = bf16[128,32]{1,0:T(8,128)(2,1)} async-done(((bf16[256,32]{1,0:T(8,128)(2,1)}), bf16[128,32]{1,0:T(8,128)(2,1)}) %reduce-scatter.45.cloned.1.call-update) | async-done | bytes 8208
  670.6 1.7 fusion.283
  672.2 23.8 %all-gather.9 = bf16[512,128]{1,0:T(8,128)(2,1)S(1)} all-gather(bf16[32,128]{1,0:T(8,128)(2,1)S(1)} %get-tuple-element.86), channel_id=11, replica_groups=mesh['layer'=4,'prow'=2,'pcol'=16] {'pcol'}, dimensions={0}, use_global_device_ids=true | all-gather | bytes 139264 | tf_op jit(solution)/shard_map/all_gather | solution.py:49
  699.5 1.3 pad_clamp_fusion.3
  700.8 10.1 %reduce-scatter.47.cloned.1.call-done = bf16[128,32]{1,0:T(8,128)(2,1)} async-done(((bf16[256,32]{1,0:T(8,128)(2,1)}), bf16[128,32]{1,0:T(8,128)(2,1)}) %reduce-scatter.47.cloned.1.call-update) | async-done | bytes 8208
  712.7 23.9 %all-gather.10 = bf16[512,128]{1,0:T(8,128)(2,1)S(1)} all-gather(bf16[32,128]{1,0:T(8,128)(2,1)S(1)} %get-tuple-element.88), channel_id=12, replica_groups=mesh['layer'=4,'prow'=2,'pcol'=16] {'pcol'}, dimensions={0}, use_global_device_ids=true | all-gather | bytes 139264 | tf_op jit(solution)/shard_map/all_gather | solution.py:49
  740.0 1.2 pad_clamp_fusion.2
  741.2 10.3 %reduce-scatter.49.cloned.1.call-done = bf16[128,32]{1,0:T(8,128)(2,1)} async-done(((bf16[256,32]{1,0:T(8,128)(2,1)}), bf16[128,32]{1,0:T(8,128)(2,1)}) %reduce-scatter.49.cloned.1.call-update) | async-done | bytes 8208
  752.4 23.9 %all-gather.11 = bf16[512,128]{1,0:T(8,128)(2,1)S(1)} all-gather(bf16[32,128]{1,0:T(8,128)(2,1)S(1)} %get-tuple-element.90), channel_id=13, replica_groups=mesh['layer'=4,'prow'=2,'pcol'=16] {'pcol'}, dimensions={0}, use_global_device_ids=true | all-gather | bytes 139264 | tf_op jit(solution)/shard_map/all_gather | solution.py:49
  779.9 1.2 pad_clamp_fusion.1
  781.1 10.2 %reduce-scatter.51.cloned.1.call-done = bf16[128,32]{1,0:T(8,128)(2,1)} async-done(((bf16[256,32]{1,0:T(8,128)(2,1)}), bf16[128,32]{1,0:T(8,128)(2,1)}) %reduce-scatter.51.cloned.1.call-update) | async-done | bytes 8208
  792.3 23.9 %all-gather.12 = bf16[512,128]{1,0:T(8,128)(2,1)S(1)} all-gather(bf16[32,128]{1,0:T(8,128)(2,1)S(1)} %get-tuple-element.92), channel_id=14, replica_groups=mesh['layer'=4,'prow'=2,'pcol'=16] {'pcol'}, dimensions={0}, use_global_device_ids=true | all-gather | bytes 139264 | tf_op jit(solution)/shard_map/all_gather | solution.py:49
  819.7 1.2 pad_clamp_fusion
  820.9 10.2 %reduce-scatter.53.cloned.1.call-done = bf16[128,32]{1,0:T(8,128)(2,1)} async-done(((bf16[256,32]{1,0:T(8,128)(2,1)}), bf16[128,32]{1,0:T(8,128)(2,1)}) %reduce-scatter.53.cloned.1.call-update) | async-done | bytes 8208
  832.1 23.9 %all-gather.13 = bf16[512,128]{1,0:T(8,128)(2,1)S(1)} all-gather(bf16[32,128]{1,0:T(8,128)(2,1)S(1)} %get-tuple-element.94), channel_id=15, replica_groups=mesh['layer'=4,'prow'=2,'pcol'=16] {'pcol'}, dimensions={0}, use_global_device_ids=true | all-gather | bytes 139264 | tf_op jit(solution)/shard_map/all_gather | solution.py:49
  859.4 1.4 maximum_bitcast_fusion
  860.8 10.1 %reduce-scatter.55.cloned.1.call-done = bf16[128,32]{1,0:T(8,128)(2,1)} async-done(((bf16[256,32]{1,0:T(8,128)(2,1)}), bf16[128,32]{1,0:T(8,128)(2,1)}) %reduce-scatter.55.cloned.1.call-update) | async-done | bytes 8208
  (170 shorter events, 56.2 us)
Async XLA Ops:
  7.2 87.2 %copy-start.4 = (f32[1,1,1,5,128,128]{5,4,3,2,1,0:T(8,128)S(1)}, f32[1,1,1,5,128,128]{5,4,3,2,1,0:T(8,128)}, u32[]{:S(2)}) copy-start(f32[1,1,1,5,128,128]{5,4,3,2,1,0:T(8,128)} %param.19) | copy-start | bytes 983044
  7.2 87.2 %copy-start.7 = (f32[1,1,1,5,32,128]{5,4,3,2,1,0:T(8,128)S(1)}, f32[1,1,1,5,32,128]{5,4,3,2,1,0:T(8,128)}, u32[]{:S(2)}) copy-start(f32[1,1,1,5,32,128]{5,4,3,2,1,0:T(8,128)} %param.18) | copy-start | bytes 245764
  7.2 92.3 %copy-start = (bf16[1,1,1,5,16,128,128]{6,5,4,3,2,1,0:T(8,128)(2,1)S(1)}, bf16[1,1,1,5,16,128,128]{6,5,4,3,2,1,0:T(8,128)(2,1)}, u32[]{:S(2)}) copy-start(bf16[1,1,1,5,16,128,128]{6,5,4,3,2,1,0:T(8,128)(2,1)} %param.21) | copy-start | bytes 7864324
  7.2 86.4 %reduce-scatter.29.cloned.1.call-start = ((), (), s32[]{:S(2)}) async-start(), calls=%async_computation.14 | async-start | bytes 557056 | tf_op jit(solution)/shard_map/reduce_scatter | solution.py:44
  18.5 154.9 %reduce-scatter.31.cloned.1.call-start = ((), (), s32[]{:S(2)}) async-start(), calls=%async_computation.15 | async-start | bytes 557056 | tf_op jit(solution)/shard_map/reduce_scatter | solution.py:44
  101.5 152.1 %reduce-scatter.33.cloned.1.call-start = ((), (), s32[]{:S(2)}) async-start(), calls=%async_computation.16 | async-start | bytes 557056 | tf_op jit(solution)/shard_map/reduce_scatter | solution.py:44
  181.9 152.1 %reduce-scatter.35.cloned.1.call-start = ((), (), s32[]{:S(2)}) async-start(), calls=%async_computation.17 | async-start | bytes 557056 | tf_op jit(solution)/shard_map/reduce_scatter | solution.py:44
  261.0 81.6 %copy-start.14 = (s32[1,1,2,16]{3,2,1,0:T(2,128)S(1)}, s32[1,1,2,16]{3,2,1,0:T(2,128)}, u32[]{:S(2)}) copy-start(s32[1,1,2,16]{3,2,1,0:T(2,128)} %param.30) | copy-start | bytes 388
  261.0 81.6 %copy-start.13 = (s32[1,1,2,16]{3,2,1,0:T(2,128)S(1)}, s32[1,1,2,16]{3,2,1,0:T(2,128)}, u32[]{:S(2)}) copy-start(s32[1,1,2,16]{3,2,1,0:T(2,128)} %param.31) | copy-start | bytes 388
  261.1 168.0 %copy-start.5 = (f32[1,1,3,128,128]{4,3,2,1,0:T(8,128)S(1)}, f32[1,1,3,128,128]{4,3,2,1,0:T(8,128)}, u32[]{:S(2)}) copy-start(f32[1,1,3,128,128]{4,3,2,1,0:T(8,128)} %param.26) | copy-start | bytes 589828
  262.2 152.2 %reduce-scatter.37.cloned.1.call-start = ((), (), s32[]{:S(2)}) async-start(), calls=%async_computation.18 | async-start | bytes 557056 | tf_op jit(solution)/shard_map/reduce_scatter | solution.py:44
  340.8 94.6 %copy-start.2 = (bf16[1,1,2,16,128,128]{5,4,3,2,1,0:T(8,128)(2,1)S(1)}, bf16[1,1,2,16,128,128]{5,4,3,2,1,0:T(8,128)(2,1)}, u32[]{:S(2)}) copy-start(bf16[1,1,2,16,128,128]{5,4,3,2,1,0:T(8,128)(2,1)} %param.28) | copy-start | bytes 3145732
  341.4 168.2 %copy-start.10 = (f32[1,1,3,32,128]{4,3,2,1,0:T(8,128)S(1)}, f32[1,1,3,32,128]{4,3,2,1,0:T(8,128)}, u32[]{:S(2)}) copy-start(f32[1,1,3,32,128]{4,3,2,1,0:T(8,128)} %param.25) | copy-start | bytes 147460
  342.5 166.2 %reduce-scatter.39.cloned.1.call-start = ((), (), s32[]{:S(2)}) async-start(), calls=%async_computation.19 | async-start | bytes 557056 | tf_op jit(solution)/shard_map/reduce_scatter | solution.py:44
  436.4 82.1 %copy-start.11 = (s32[1,1,1,5,16]{4,2,3,1,0:T(1,128)S(1)}, s32[1,1,1,5,16]{4,2,3,1,0:T(1,128)}, u32[]{:S(2)}) copy-start(s32[1,1,1,5,16]{4,2,3,1,0:T(1,128)} %param.23) | copy-start | bytes 964
  436.4 82.7 %copy-start.12 = (s32[1,1,1,5,16]{4,2,3,1,0:T(1,128)S(1)}, s32[1,1,1,5,16]{4,2,3,1,0:T(1,128)}, u32[]{:S(2)}) copy-start(s32[1,1,1,5,16]{4,2,3,1,0:T(1,128)} %param.24) | copy-start | bytes 964
  436.4 153.6 %copy-start.6 = (f32[1,1,3,128,128]{4,3,2,1,0:T(8,128)S(1)}, f32[1,1,3,128,128]{4,3,2,1,0:T(8,128)}, u32[]{:S(2)}) copy-start(f32[1,1,3,128,128]{4,3,2,1,0:T(8,128)} %param.27) | copy-start | bytes 589828
  437.5 151.5 %reduce-scatter.41.cloned.1.call-start = ((), (), s32[]{:S(2)}) async-start(), calls=%async_computation.20 | async-start | bytes 557056 | tf_op jit(solution)/shard_map/reduce_scatter | solution.py:44
  517.3 110.9 %reduce-scatter.43.cloned.1.call-start = ((), (), s32[]{:S(2)}) async-start(), calls=%async_computation.21 | async-start | bytes 98304
  613.8 82.9 %copy-start.1 = (bf16[1,1,1,5,16,128,128]{6,5,4,3,2,1,0:T(8,128)(2,1)S(1)}, bf16[1,1,1,5,16,128,128]{6,5,4,3,2,1,0:T(8,128)(2,1)}, u32[]{:S(2)}) copy-start(bf16[1,1,1,5,16,128,128]{6,5,4,3,2,1,0:T(8,128)(2,1)} %param.22) | copy-start | bytes 7864324
  616.3 95.4 %copy-start.3 = (f32[1,1,1,5,128,128]{5,4,3,2,1,0:T(8,128)S(1)}, f32[1,1,1,5,128,128]{5,4,3,2,1,0:T(8,128)}, u32[]{:S(2)}) copy-start(f32[1,1,1,5,128,128]{5,4,3,2,1,0:T(8,128)} %param.20) | copy-start | bytes 983044
  617.1 52.7 %reduce-scatter.45.cloned.1.call-start = ((), (), s32[]{:S(2)}) async-start(), calls=%async_computation.22 | async-start | bytes 98304
  657.5 94.8 %copy-start.9 = (f32[32,128]{1,0:T(8,128)S(1)}, f32[32,128]{1,0:T(8,128)}, u32[]{:S(2)}) copy-start(f32[32,128]{1,0:T(8,128)} %get-tuple-element.75) | copy-start | bytes 49156
  658.3 52.7 %reduce-scatter.47.cloned.1.call-start = ((), (), s32[]{:S(2)}) async-start(), calls=%async_computation.23 | async-start | bytes 98304
  698.7 93.4 %copy-start.8 = (f32[32,128]{1,0:T(8,128)S(1)}, f32[32,128]{1,0:T(8,128)}, u32[]{:S(2)}) copy-start(f32[32,128]{1,0:T(8,128)} %get-tuple-element.73) | copy-start | bytes 49156
  699.5 52.0 %reduce-scatter.49.cloned.1.call-start = ((), (), s32[]{:S(2)}) async-start(), calls=%async_computation.24 | async-start | bytes 98304
  740.0 51.3 %reduce-scatter.51.cloned.1.call-start = ((), (), s32[]{:S(2)}) async-start(), calls=%async_computation.25 | async-start | bytes 98304
  779.8 51.3 %reduce-scatter.53.cloned.1.call-start = ((), (), s32[]{:S(2)}) async-start(), calls=%async_computation.26 | async-start | bytes 98304
  819.6 51.3 %reduce-scatter.55.cloned.1.call-start = ((), (), s32[]{:S(2)}) async-start(), calls=%async_computation.27 | async-start | bytes 98304
  872.7 0.6 copy-start.15
Sparse Core Ops, SparseCore 0:
  18.6 74.9 reduce-scatter.28
  101.6 71.6 reduce-scatter.30
  182.0 71.6 reduce-scatter.32
  262.3 71.6 reduce-scatter.34
  342.7 71.6 reduce-scatter.36
  437.6 71.0 reduce-scatter.38
  517.4 71.5 reduce-scatter.40
  617.2 10.9 reduce-scatter.42
  658.4 11.3 reduce-scatter.44
  699.6 11.2 reduce-scatter.46
  740.1 11.3 reduce-scatter.48
  780.0 11.2 reduce-scatter.50
  819.7 11.3 reduce-scatter.52
  859.6 11.2 reduce-scatter.54
where the time goes:
time: 882 us; the launch traced here: 880 us
  waiting for transfers between devices  574 us (65%)
  blocking collectives  210 us (24%)
  local copies, waits for them, and re-layouts  34.7 us (4%)
  matrix products  34.2 us (4%)
  between operations  14.6 us (2%)
  other arithmetic  11.1 us (1%)
    reduce_scatter x7, waiting for transfers between devices, column_reduce(): lax.psum_scatter(flat_shares, 'pcol', scatter_dimension=1, tiled=True)  503 us
    all_gather x7, blocking collectives, gather_solution(): lax.all_gather(values.astype(jnp.bfloat16)[None], 'pcol', axis=0, tiled=T...  166 us
    unnamed x21, waiting for transfers between devices  71.6 us
    all_gather x7, blocking collectives, lower_terms(): lax.all_gather(values.astype(jnp.bfloat16)[None], 'prow', axis=0, tiled=T...  30.5 us
    unnamed x57, local copies, waits for them, and re-layouts  19.3 us
  transfers between devices with their start and end apart: 14, of which 14 were waited for; matrix products, arithmetic and copies ran while one was open for 1% of the time, Pallas kernels for 0%

commit v1 on v0

v1 whole, which is shorter than its diff:
```python
import jax
import jax.numpy as jnp
from jax import lax
from jax.experimental import pallas as pl
from jax.experimental.pallas import tpu as pltpu
from jax.sharding import PartitionSpec as P

MESH = pl.DeviceIdType.MESH
F32 = jnp.float32
BF16 = jnp.bfloat16
SUB, TOP, SLOTS, COLS, SIDES, WIDTH = 5, 3, 16, 16, 32, 128
HALF = SIDES // 2
LINKED = SUB + TOP - 1
ORDER = (10, 9, 11, 6, 14, 5, 7, 13, 15, 8, 2, 1, 3, 4, 12, 0)


def dot(a, b):
    return jnp.dot(a, b, preferred_element_type=F32)


def dot_full(a, b):
    return jnp.dot(a, b, preferred_element_type=F32, precision=lax.Precision.HIGHEST)


def dot_split(a, b):
    high = a.astype(BF16)
    low = (a - high.astype(F32)).astype(BF16)
    return dot(high, b) + dot(low, b)


def wait_for(ref, sem):
    pltpu.make_async_copy(ref, ref, sem).wait()


def kernel(
    sub_rhs, sub_linv, sub_uinv, sub_lower, sub_upper, sub_src, sub_tgt,
    top_rhs, top_linv, top_uinv, top_lower, top_upper, top_src, top_tgt,
    sub_out, top_out,
    lower, upper, linv, uinv, rhs_sub, rhs_top,
    linv_low, uinv_low, linv_other, uinv_other, rhs_sub_other, rhs_top_other,
    perm, psrc, ends,
    ylow, ylow_other, y_sub, y_top, sums, pend, pend_top,
    send_f, recv_f, send_ft, recv_5, recv_ft,
    halves, core_out, core_in, six,
    x_sub, x_top, send_b, recv_b, send_bt, recv_7, recv_6, recv_b5, six_in, six_out, last_out, last_in, top_mine, top_other,
    load_sem, lin_sem, misc_recv, misc_send, rf_sem, sf_sem, rb_sem, sb_sem,
):
    l, r, c = lax.axis_index("layer"), lax.axis_index("prow"), lax.axis_index("pcol")
    high, half = l // 2, l % 2
    half_rows = pl.ds(pl.multiple_of(half * HALF, HALF), HALF)
    me = r * COLS + c

    loads = (
        (sub_lower, lower.at[pl.ds(0, SUB)]),
        (top_lower, lower.at[pl.ds(SUB, TOP - 1)]),
        (sub_upper, upper.at[pl.ds(0, SUB)]),
        (top_upper, upper.at[pl.ds(SUB, TOP - 1)]),
        (sub_linv, linv.at[pl.ds(0, SUB)]),
        (top_linv, linv.at[pl.ds(SUB, TOP)]),
        (sub_uinv, uinv.at[pl.ds(0, SUB)]),
        (top_uinv, uinv.at[pl.ds(SUB, TOP)]),
        (sub_rhs, rhs_sub),
        (top_rhs.at[:, half_rows], rhs_top),
    )
    copies = [pltpu.make_async_copy(a, b, load_sem.at[i]) for i, (a, b) in enumerate(loads)]
    for i in (8, 4, 5, 6, 7, 9, 0, 1, 2, 3):
        copies[i].start()

    barrier = pltpu.get_barrier_semaphore()
    for flip in (0, 1, 2):
        for j in range(2):
            for i in range(COLS):
                if flip or j or i:
                    pl.semaphore_signal(barrier, inc=1, device_id=(l ^ flip, r ^ j, c ^ i), device_id_type=MESH)

    def sort_level(src, tgt, row, t):
        codes = [tgt[row, k] for k in range(SLOTS)]
        rank = [jnp.int32(0)] * SLOTS
        for k in range(SLOTS):
            for j in range(k):
                before = (codes[j] <= codes[k]).astype(jnp.int32)
                rank[k] = rank[k] + before
                rank[j] = rank[j] + (1 - before)
        for i in range(SLOTS):
            slot = jnp.int32(0)
            for k in range(1, SLOTS):
                slot = slot + jnp.where(rank[k] == i, k, 0)
            perm[t, i] = slot
            psrc[t, i] = src[row, slot]
        ends[t, 0] = 0
        for q in range(2 * COLS):
            count = jnp.int32(0)
            for k in range(SLOTS):
                count = count + (codes[k] <= q).astype(jnp.int32)
            ends[t, q + 1] = count

    @pl.loop(0, SUB)
    def _(t):
        sort_level(sub_src, sub_tgt, t, t)

    @pl.loop(0, TOP - 1)
    def _(t):
        sort_level(top_src, top_tgt, t, t + SUB)

    copies[8].wait()
    copies[4].wait()
    y0 = dot_full(rhs_sub[0], linv[0])
    y_sub[0] = y0
    ylow[r] = y0.astype(BF16)
    for i in (5, 6, 7, 9, 0, 1, 2, 3):
        copies[i].wait()

    @pl.loop(0, 6)
    def _(t):
        linv_low[t] = linv[t + 1].astype(BF16)
        uinv_low[t] = uinv[t + 1].astype(BF16)

    @pl.loop(0, COLS)
    def _(q):
        pend[q] = jnp.zeros((SIDES, WIDTH), F32)

    pl.semaphore_wait(barrier, 95)

    def to(device, src, dst, send_sem, recv_sem):
        copy = pltpu.make_async_remote_copy(
            src_ref=src, dst_ref=dst, send_sem=send_sem, recv_sem=recv_sem, device_id=device, device_id_type=MESH
        )
        copy.start()
        return copy

    other_row = (l, 1 - r, c)
    other_core = (l ^ 1, r, c)
    other_high = (l ^ 2, r, c)

    first = to(other_row, ylow.at[r], ylow_other, misc_send.at[0], misc_recv.at[0])
    lin_copies = [
        to(other_row, linv_low.at[t], linv_other.at[t], lin_sem.at[0, t], lin_sem.at[1, t]) for t in range(6)
    ]
    rhs_copy = to(
        other_row, rhs_sub.at[pl.ds(1, SUB - 1)], rhs_sub_other, misc_send.at[1], misc_recv.at[1]
    )
    rhs_top_copy = to(other_row, rhs_top.at[pl.ds(0, 2)], rhs_top_other, misc_send.at[2], misc_recv.at[2])

    def wait_linv(t):
        wait_for(linv_other.at[t - 1], lin_sem.at[1, t - 1])

    def products(t, rows):
        total = jnp.zeros((rows, WIDTH), F32)
        sums[0, :rows] = total
        for i in range(SLOTS):
            value = ylow[psrc[t, i]]
            total = total + dot(value[:rows], lower[t, perm[t, i]])
            sums[i + 1, :rows] = total

    def share(t, code, rows):
        return sums[ends[t, code + 1], :rows] - sums[ends[t, code], :rows]

    def forward(t):
        products(t, SIDES)
        for i in ORDER:
            q = c ^ i
            send_f[t, q] = (share(t, q, SIDES) + pend[q]).astype(BF16)
            for j in (1, 0):
                if i or j:
                    to((l, r ^ j, q), send_f.at[t, q], recv_f.at[t, me], sf_sem.at[t], rf_sem.at[t + 1])
        recv_f[t, me] = send_f[t, c]
        for q in range(COLS):
            pend[q] = share(t, COLS + q, SIDES)

    def add_up(ref, rows):
        parts = [ref[i].astype(F32) for i in range(COLS)]
        while len(parts) > 1:
            parts = [a + b for a, b in zip(parts[::2], parts[1::2])]
        return parts[0]

    def arrive(t):
        wait_for(recv_f.at[t - 1, pl.ds(0, 2 * COLS - 1)], rf_sem.at[t])
        wait_linv(t)
        mine = rhs_sub[t] - add_up(recv_f.at[t - 1, pl.ds(r * COLS, COLS)], SIDES)
        others = rhs_sub_other[t - 1] - add_up(recv_f.at[t - 1, pl.ds((1 - r) * COLS, COLS)], SIDES)
        y = dot_full(mine, linv[t])
        y_sub[t] = y
        ylow[r] = y.astype(BF16)
        ylow[1 - r] = dot_split(others, linv_other[t - 1]).astype(BF16)

    first.wait_recv()
    first.wait_send()
    ylow[1 - r] = ylow_other[...]
    forward(0)
    rhs_copy.wait_recv()

    @pl.loop(1, SUB - 1)
    def _(t):
        arrive(t)
        forward(t)

    t = SUB - 1
    arrive(t)
    products(t, SIDES)
    for q in range(COLS):
        both = share(t, q, SIDES) + pend[q]
        halves[0, 0, q] = both[:HALF]
        halves[0, 1, q] = both[HALF:]
    core_out[0] = halves[0, 1 - half].astype(BF16)
    core_copies = [to(other_core, core_out.at[0], core_in.at[0], misc_send.at[3], misc_recv.at[3])]
    for q in range(COLS):
        both = share(t, COLS + q, SIDES)
        halves[1, 0, q] = both[:HALF]
        halves[1, 1, q] = both[HALF:]
    core_out[1] = halves[1, 1 - half].astype(BF16)
    core_copies.append(to(other_core, core_out.at[1], core_in.at[1], misc_send.at[4], misc_recv.at[4]))
    core_copies[0].wait_recv()
    slot_5 = high * 2 * COLS + me
    for i in ORDER:
        q = c ^ i
        send_ft[0, q] = (halves[0, half, q] + core_in[0, q].astype(F32)).astype(BF16)
        for flip in (2, 0):
            for j in (1, 0):
                if i or j or flip:
                    to((l ^ flip, r ^ j, q), send_ft.at[0, q], recv_5.at[slot_5], sf_sem.at[t], rf_sem.at[t + 1])
    recv_5[slot_5] = send_ft[0, c]
    core_copies[1].wait_recv()
    six[high] = (halves[1, half] + core_in[1].astype(F32)).astype(BF16)
    six_copy = to(other_high, six.at[high], six.at[high], misc_send.at[5], misc_recv.at[5])
    upper_copy = to(other_row, uinv_low, uinv_other, misc_send.at[6], misc_recv.at[6])
    rhs_top_copy.wait_recv()
    six_copy.wait_recv()
    for q in range(COLS):
        pend_top[q] = six[0, q].astype(F32) + six[1, q].astype(F32)

    def arrive_top(t, mine, others):
        y = dot_full(rhs_top[t] - mine, linv[t + SUB])
        y_top[t] = y
        if t < TOP - 1:
            wait_linv(t + SUB)
            ylow[r, :HALF] = y.astype(BF16)
            ylow[1 - r, :HALF] = dot_split(rhs_top_other[t] - others, linv_other[t + SUB - 1]).astype(BF16)

    def forward_top(t):
        products(t + SUB, HALF)
        for i in ORDER:
            q = c ^ i
            value = share(t + SUB, q, HALF) + pend_top[q]
            send_ft[t + 1, q] = value.astype(BF16)
            for j in (1, 0):
                if i or j:
                    to((l, r ^ j, q), send_ft.at[t + 1, q], recv_ft.at[t, me], sf_sem.at[t + SUB], rf_sem.at[t + SUB + 1])
        recv_ft[t, me] = send_ft[t + 1, c]
        if t == 0:
            for q in range(COLS):
                pend_top[q] = share(t + SUB, COLS + q, HALF)

    wait_for(recv_5.at[pl.ds(0, 4 * COLS - 1)], rf_sem.at[SUB])

    def add_up_5(row):
        return add_up(recv_5.at[pl.ds(row * COLS, COLS)], HALF) + add_up(
            recv_5.at[pl.ds((2 + row) * COLS, COLS)], HALF
        )

    arrive_top(0, add_up_5(r), add_up_5(1 - r))
    forward_top(0)
    for t in (1, 2):
        wait_for(recv_ft.at[t - 1, pl.ds(0, 2 * COLS - 1)], rf_sem.at[t + SUB])
        mine = add_up(recv_ft.at[t - 1, pl.ds(r * COLS, COLS)], HALF)
        if t == 1:
            arrive_top(1, mine, add_up(recv_ft.at[t - 1, pl.ds((1 - r) * COLS, COLS)], HALF))
            forward_top(1)
        else:
            arrive_top(2, mine, None)

    x7 = dot_full(y_top[2], uinv[7])
    top_mine[2] = x7
    send_bt[2, 0] = x7.astype(BF16)
    for i in ORDER:
        if i:
            to((l, r, c ^ i), send_bt.at[2, 0], recv_7.at[c], sb_sem.at[7], rb_sem.at[7])
    recv_7[c] = send_bt[2, 0]
    upper_copy.wait_recv()
    wait_for(recv_7.at[pl.ds(0, COLS - 1)], rb_sem.at[7])
    x_top[pl.ds(COLS, COLS)] = recv_7[...]

    def down(t, load, src, row):
        total = None
        for k in range(SLOTS):
            value = dot(load(k), upper[t, k])
            taken = value * src[row, k].astype(F32)
            total = value if total is None else total + value
            second = taken if k == 0 else second + taken
        at_first = r == 0
        parts = (total - second, second)
        return jnp.where(at_first, parts[0], parts[1]), jnp.where(at_first, parts[1], parts[0])

    def parts_of(t, mine, others, y):
        a = dot_full(y - mine, uinv[t])
        b = -dot_split(others, uinv_other[t - 1])
        return a, b

    mine, others = down(6, lambda k: x_top[COLS + top_tgt[1, k] % COLS], top_src, 1)
    a, b = parts_of(6, mine, others, y_top[1])
    top_mine[1] = a
    send_bt[1, 0] = a.astype(BF16)
    send_bt[1, 1] = b.astype(BF16)
    for i in ORDER:
        to((l, 1 - r, c ^ i), send_bt.at[1, 1], recv_6.at[COLS + c], sb_sem.at[6], rb_sem.at[6])
        if i:
            to((l, r, c ^ i), send_bt.at[1, 0], recv_6.at[c], sb_sem.at[6], rb_sem.at[6])
    recv_6[c] = send_bt[1, 0]
    wait_for(recv_6.at[pl.ds(0, 2 * COLS - 1)], rb_sem.at[6])
    for q in range(COLS):
        x_top[q] = (recv_6[q].astype(F32) + recv_6[COLS + q].astype(F32)).astype(BF16)
    top_mine[1] = top_mine[1] + recv_6[COLS + c].astype(F32)
    six_out[...] = x_top[pl.ds(0, COLS)]
    x6_copy = to(other_core, six_out, six_in, misc_send.at[7], misc_recv.at[7])

    mine, others = down(5, lambda k: x_top[top_tgt[0, k]], top_src, 0)
    a, b = parts_of(5, mine, others, y_top[0])
    top_mine[0] = a
    send_bt[0, 0] = a.astype(BF16)
    send_bt[0, 1] = b.astype(BF16)
    slot_a = half * 2 * COLS + c
    for i in ORDER:
        for flip in (1, 0):
            to((l ^ flip, 1 - r, c ^ i), send_bt.at[0, 1], recv_b5.at[slot_a + COLS], sb_sem.at[5], rb_sem.at[5])
            if i or flip:
                to((l ^ flip, r, c ^ i), send_bt.at[0, 0], recv_b5.at[slot_a], sb_sem.at[5], rb_sem.at[5])
    recv_b5[slot_a] = send_bt[0, 0]
    x6_copy.wait_recv()
    for q in range(COLS):
        x_sub[6 * COLS + q, half] = x_top[q]
        x_sub[6 * COLS + q, 1 - half] = six_in[q]
    wait_for(recv_b5.at[pl.ds(0, 4 * COLS - 1)], rb_sem.at[5])
    for q in range(COLS):
        for h in range(2):
            x_sub[5 * COLS + q, h] = (
                recv_b5[h * 2 * COLS + q].astype(F32) + recv_b5[h * 2 * COLS + COLS + q].astype(F32)
            ).astype(BF16)
    top_mine[0] = top_mine[0] + recv_b5[slot_a + COLS].astype(F32)
    top_copy = to(other_core, top_mine, top_other, misc_send.at[8], misc_recv.at[8])

    def down_sub(t):
        return down(
            t,
            lambda k: x_sub[(t + 1) * COLS + sub_tgt[t, k]].reshape(SIDES, WIDTH),
            sub_src,
            t,
        )

    @pl.loop(0, SUB - 1)
    def _(step):
        t = SUB - 1 - step
        mine, others = down_sub(t)
        a, b = parts_of(t, mine, others, y_sub[t])
        send_b[t, 0] = a.astype(BF16)
        send_b[t, 1] = b.astype(BF16)
        for i in ORDER:
            to((l, 1 - r, c ^ i), send_b.at[t, 1], recv_b.at[t, COLS + c], sb_sem.at[t], rb_sem.at[t])
            if i:
                to((l, r, c ^ i), send_b.at[t, 0], recv_b.at[t, c], sb_sem.at[t], rb_sem.at[t])
        recv_b[t, c] = send_b[t, 0]
        wait_for(recv_b.at[t, pl.ds(0, 2 * COLS - 1)], rb_sem.at[t])
        for q in range(COLS):
            x = (recv_b[t, q].astype(F32) + recv_b[t, COLS + q].astype(F32)).astype(BF16)
            x_sub[t * COLS + q] = x.reshape(2, HALF, WIDTH)
        sub_out[t] = a + recv_b[t, COLS + c].astype(F32)

    mine, others = down_sub(0)
    last_out[...] = others
    last = to(other_row, last_out, last_in, misc_send.at[9], misc_recv.at[9])
    top_copy.wait_recv()
    for t in range(TOP):
        top_out[t, half_rows] = top_mine[t]
        top_out[t, pl.ds(pl.multiple_of((1 - half) * HALF, HALF), HALF)] = top_other[t]

    for copy in lin_copies + [rhs_copy, rhs_top_copy, *core_copies, six_copy, upper_copy, x6_copy, top_copy]:
        copy.wait_send()
    for t in range(SUB - 1):
        wait_for(recv_f.at[t, pl.ds(0, 2 * COLS - 1)], sf_sem.at[t])
    wait_for(recv_5.at[pl.ds(0, 4 * COLS - 1)], sf_sem.at[4])
    wait_for(recv_ft.at[0, pl.ds(0, 2 * COLS - 1)], sf_sem.at[5])
    wait_for(recv_ft.at[1, pl.ds(0, 2 * COLS - 1)], sf_sem.at[6])
    wait_for(recv_7.at[pl.ds(0, COLS - 1)], sb_sem.at[7])
    wait_for(recv_6.at[pl.ds(0, 2 * COLS - 1)], sb_sem.at[6])
    wait_for(recv_b5.at[pl.ds(0, 4 * COLS - 1)], sb_sem.at[5])
    for t in range(1, SUB):
        wait_for(recv_b.at[t, pl.ds(0, 2 * COLS - 1)], sb_sem.at[t])
    last.wait_send()
    last.wait_recv()
    sub_out[0] = dot_full(y_sub[0] - mine - last_in[...], uinv[0])


def local(*args):
    flat = [a.reshape(a.shape[3:] if i < 7 else a.shape[2:]) for i, a in enumerate(args)]
    vmem, smem, dma = pltpu.VMEM, pltpu.SMEM, pltpu.SemaphoreType.DMA
    tile = (SIDES, WIDTH)
    half = (HALF, WIDTH)
    block = (WIDTH, WIDTH)
    scratch = [
        vmem((LINKED, SLOTS) + block, BF16),
        vmem((LINKED, SLOTS) + block, BF16),
        vmem((SUB + TOP,) + block, F32),
        vmem((SUB + TOP,) + block, F32),
        vmem((SUB,) + tile, F32),
        vmem((TOP,) + half, F32),
        vmem((6,) + block, BF16),
        vmem((6,) + block, BF16),
        vmem((6,) + block, BF16),
        vmem((6,) + block, BF16),
        vmem((SUB - 1,) + tile, F32),
        vmem((2,) + half, F32),
        smem((LINKED, SLOTS), jnp.int32),
        smem((LINKED, SLOTS), jnp.int32),
        smem((LINKED, 2 * COLS + 1), jnp.int32),
        vmem((2,) + tile, BF16),
        vmem(tile, BF16),
        vmem((SUB,) + tile, F32),
        vmem((TOP,) + half, F32),
        vmem((SLOTS + 1,) + tile, F32),
        vmem((COLS,) + tile, F32),
        vmem((COLS,) + half, F32),
        vmem((SUB - 1, COLS) + tile, BF16),
        vmem((SUB - 1, 2 * COLS) + tile, BF16),
        vmem((TOP, COLS) + half, BF16),
        vmem((4 * COLS,) + half, BF16),
        vmem((2, 2 * COLS) + half, BF16),
        vmem((2, 2, COLS) + half, F32),
        vmem((2, COLS) + half, BF16),
        vmem((2, COLS) + half, BF16),
        vmem((2, COLS) + half, BF16),
        vmem((7 * COLS, 2) + half, BF16),
        vmem((2 * COLS,) + half, BF16),
        vmem((SUB, 2) + tile, BF16),
        vmem((SUB, 2 * COLS) + tile, BF16),
        vmem((TOP, 2) + half, BF16),
        vmem((COLS,) + half, BF16),
        vmem((2 * COLS,) + half, BF16),
        vmem((4 * COLS,) + half, BF16),
        vmem((COLS,) + half, BF16),
        vmem((COLS,) + half, BF16),
        vmem(tile, F32),
        vmem(tile, F32),
        vmem((TOP,) + half, F32),
        vmem((TOP,) + half, F32),
        dma((10,)),
        dma((2, 6)),
        dma((10,)),
        dma((10,)),
        dma((SUB + TOP,)),
        dma((SUB + TOP,)),
        dma((SUB + TOP,)),
        dma((SUB + TOP,)),
    ]
    any_spec = pl.BlockSpec(memory_space=pl.ANY)
    smem_spec = pl.BlockSpec(memory_space=pltpu.SMEM)
    vmem_spec = pl.BlockSpec(memory_space=pltpu.VMEM)
    sub, top = pl.pallas_call(
        kernel,
        out_shape=(
            jax.ShapeDtypeStruct((SUB,) + tile, F32),
            jax.ShapeDtypeStruct((TOP,) + tile, F32),
        ),
        in_specs=([any_spec] * 5 + [smem_spec] * 2) * 2,
        out_specs=(vmem_spec, vmem_spec),
        scratch_shapes=scratch,
        compiler_params=pltpu.CompilerParams(
            collective_id=0, has_side_effects=True, vmem_limit_bytes=40 * 1024 * 1024
        ),
    )(*flat)
    return sub[None, None, None], top[None, None]


def solution(mesh):
    sub = P("layer", "prow", "pcol")
    top = P("prow", "pcol")
    return jax.shard_map(
        local, mesh=mesh, in_specs=(sub,) * 7 + (top,) * 7, out_specs=(sub, top), check_vma=False
    )
```

time: 882 us -> 127 us (0.14)
  waiting for transfers between devices: 574 us -> 0 us
  blocking collectives: 210 us -> 0 us
  Pallas kernels: 0 us -> 111 us
  matrix products: 34.2 us -> 0 us
  local copies, waits for them, and re-layouts: 34.7 us -> 14.7 us
  between operations: 14.6 us -> 0.65 us
  other arithmetic: 11.1 us -> 0 us
    reduce_scatter x7 -> x0, waiting for transfers between devices: 503 us -> none  [column_reduce(): lax.psum_scatter(flat_shares, 'pcol', scatter_dimension=1, tiled=True)]
    all_gather x14 -> x0, blocking collectives: 197 us -> none  [the longest x7 166 us: gather_solution(): lax.all_gather(values.astype(jnp.bfloat16)[None], 'pcol', axis=0, tiled=T...]
    pallas_call x0 -> x1, Pallas kernels: none -> 111 us  [local(): pl.pallas_call(kernel, out_shape=(jax.ShapeDtypeStruct((SUB,) + tile, F32...]
    unnamed x21 -> x0, waiting for transfers between devices: 71.6 us -> none
    dot_general x44 -> x0, matrix products: 34.2 us -> none  [the longest x16 13 us: apply_inverse(): jnp.dot(remainder, inverse, precision=lax.Precision.HIGHEST, preferred_el...]
    psum x1 -> x0, blocking collectives: 13.8 us -> none  [local(): lax.psum(ancestral[0].astype(jnp.bfloat16), 'layer').astype(jnp.float32)]
    unnamed x57 -> x27, local copies, waits for them, and re-layouts: 19.3 us -> 14.7 us
  transfers between devices with their start and end apart: 14 -> 0, of which waited for: 14 -> 0; matrix products, arithmetic and copies ran while one was open for 1% -> 0% of each run, Pallas kernels for 0% -> 0%
where the time goes in v1:
time: 127 us; the launch traced here: 126 us
  Pallas kernels  111 us (87%)
  local copies, waits for them, and re-layouts  14.7 us (12%)
    pallas_call x1, Pallas kernels, local(): pl.pallas_call(kernel, out_shape=(jax.ShapeDtypeStruct((SUB,) + tile, F32...  111 us
    unnamed x27, local copies, waits for them, and re-layouts  14.7 us

profile of v1, /device:TPU:0, one launch (start us, length us, event | category | flops | bytes accessed | tf_op | source)
XLA Modules:
  0.0 126.1 jit_solution(2490536531153919959)
XLA Ops:
  0.6 0.7 copy_bitcast_fusion
  1.3 0.0 copy-start
  1.3 1.7 %copy-done = bf16[1,1,1,5,16,128,128]{6,5,4,3,2,1,0:T(8,128)(2,1)S(1)} copy-done((bf16[1,1,1,5,16,128,128]{6,5,4,3,2,1,0:T(8,128)(2,1)S(1)}, bf16[1,1,1,5,16,128,128]{6,5,4,3,2,1,0:T(8,128)(2,1)}, u32[]{:S(2)}) %copy-start) | copy-done | bytes 2621464
  3.1 0.0 copy-start.1
  3.1 1.7 %copy-done.1 = bf16[1,1,1,5,16,128,128]{6,5,4,3,2,1,0:T(8,128)(2,1)S(1)} copy-done((bf16[1,1,1,5,16,128,128]{6,5,4,3,2,1,0:T(8,128)(2,1)S(1)}, bf16[1,1,1,5,16,128,128]{6,5,4,3,2,1,0:T(8,128)(2,1)}, u32[]{:S(2)}) %copy-start.1) | copy-done | bytes 2621464
  4.8 0.0 copy-start.2
  4.8 1.2 copy-done.2
  6.0 0.0 copy-start.3
  6.0 1.2 copy-done.3
  7.3 0.0 copy-start.4
  7.3 1.0 copy-done.4
  8.2 0.0 copy-start.5
  8.2 1.0 copy-done.5
  9.2 0.0 copy-start.6
  9.2 0.9 copy-done.6
  10.1 0.0 copy-start.7
  10.1 0.9 copy-done.7
  11.1 0.0 copy-start.8
  11.1 0.9 copy-done.8
  12.0 0.0 copy-start.9
  12.0 0.8 copy-done.9
  12.8 0.0 copy-start.10
  12.8 0.7 copy-done.10
  13.4 0.0 copy-start.11
  13.4 0.7 copy-done.11
  14.1 110.8 %shard_map.149 = (f32[5,32,128]{2,1,0:T(8,128)S(1)}, f32[3,32,128]{2,1,0:T(8,128)S(1)}) custom-call(f32[5,32,128]{2,1,0:T(8,128)S(1)} %bitcast.26, f32[5,128,128]{2,1,0:T(8,128)S(1)} %bitcast.22, f32[5,128,128]{2,1,0:T(8,128)S(1)} %bitcast.23, bf16[5,16,128,128]{3,2,1,0:T(8,128)(2,1)S(1)} %bitcast.18, bf16[5,16,128,128]{3,2,1,0:T(8,128)(2,1)S(1)} %bitcast.19, ...), custom_call_target="tpu_custom_call" | custom-call | tf_op jit(solution)/shard_map/pallas_call | solution.py:455
  124.9 0.6 copy.22
  125.5 0.6 copy.23
Async XLA Ops:
  1.3 1.7 %copy-start = (bf16[1,1,1,5,16,128,128]{6,5,4,3,2,1,0:T(8,128)(2,1)S(1)}, bf16[1,1,1,5,16,128,128]{6,5,4,3,2,1,0:T(8,128)(2,1)}, u32[]{:S(2)}) copy-start(bf16[1,1,1,5,16,128,128]{6,5,4,3,2,1,0:T(8,128)(2,1)} %param.17) | copy-start | bytes 7864324
  3.1 1.7 %copy-start.1 = (bf16[1,1,1,5,16,128,128]{6,5,4,3,2,1,0:T(8,128)(2,1)S(1)}, bf16[1,1,1,5,16,128,128]{6,5,4,3,2,1,0:T(8,128)(2,1)}, u32[]{:S(2)}) copy-start(bf16[1,1,1,5,16,128,128]{6,5,4,3,2,1,0:T(8,128)(2,1)} %param.18) | copy-start | bytes 7864324
  4.8 1.2 copy-start.2
  6.0 1.2 copy-start.3
  7.3 1.0 copy-start.4
  8.2 1.0 copy-start.5
  9.2 0.9 copy-start.6
  10.1 0.9 copy-start.7
  11.1 0.9 copy-start.8
  12.0 0.8 copy-start.9
  12.8 0.7 copy-start.10
  13.4 0.7 copy-start.11

commit v2 on v1

--- a/solution.py
+++ b/solution.py
@@ -33,9 +33,10 @@
 
 
 def kernel(
-    sub_rhs, sub_linv, sub_uinv, sub_lower, sub_upper, sub_src, sub_tgt,
-    top_rhs, top_linv, top_uinv, top_lower, top_upper, top_src, top_tgt,
+    sub_rhs, sub_linv, sub_uinv, sub_lower, sub_upper, sub_src_in, sub_tgt_in,
+    top_rhs, top_linv, top_uinv, top_lower, top_upper, top_src_in, top_tgt_in,
     sub_out, top_out,
+    sub_src, sub_tgt, top_src, top_tgt,
     lower, upper, linv, uinv, rhs_sub, rhs_top,
     linv_low, uinv_low, linv_other, uinv_other, rhs_sub_other, rhs_top_other,
     perm, psrc, ends,
@@ -43,7 +44,7 @@
     send_f, recv_f, send_ft, recv_5, recv_ft,
     halves, core_out, core_in, six,
     x_sub, x_top, send_b, recv_b, send_bt, recv_7, recv_6, recv_b5, six_in, six_out, last_out, last_in, top_mine, top_other,
-    load_sem, lin_sem, misc_recv, misc_send, rf_sem, sf_sem, rb_sem, sb_sem,
+    load_sem, lin_sem, group_sem, misc_recv, misc_send, rf_sem, sf_sem, rb_sem, sb_sem,
 ):
     l, r, c = lax.axis_index("layer"), lax.axis_index("prow"), lax.axis_index("pcol")
     high, half = l // 2, l % 2
@@ -61,20 +62,25 @@
         (top_uinv, uinv.at[pl.ds(SUB, TOP)]),
         (sub_rhs, rhs_sub),
         (top_rhs.at[:, half_rows], rhs_top),
+        (sub_src_in, sub_src),
+        (sub_tgt_in, sub_tgt),
+        (top_src_in, top_src),
+        (top_tgt_in, top_tgt),
     )
     copies = [pltpu.make_async_copy(a, b, load_sem.at[i]) for i, (a, b) in enumerate(loads)]
-    for i in (8, 4, 5, 6, 7, 9, 0, 1, 2, 3):
+    for i in (8, 4, 10, 11, 12, 13, 0, 5, 9, 6, 7, 1, 2, 3):
         copies[i].start()
 
     barrier = pltpu.get_barrier_semaphore()
-    for flip in (0, 1, 2):
-        for j in range(2):
-            for i in range(COLS):
-                if flip or j or i:
-                    pl.semaphore_signal(barrier, inc=1, device_id=(l ^ flip, r ^ j, c ^ i), device_id_type=MESH)
+    for flip in (1, 2):
+        pl.semaphore_signal(barrier, inc=1, device_id=(l ^ flip, r, c), device_id_type=MESH)
+    for i in ORDER:
+        for j in (1, 0):
+            if j or i:
+                pl.semaphore_signal(barrier, inc=1, device_id=(l, r ^ j, c ^ i), device_id_type=MESH)
 
     def sort_level(src, tgt, row, t):
-        codes = [tgt[row, k] for k in range(SLOTS)]
+        codes = [tgt[(*row, k)] for k in range(SLOTS)]
         rank = [jnp.int32(0)] * SLOTS
         for k in range(SLOTS):
             for j in range(k):
@@ -86,7 +92,7 @@
             for k in range(1, SLOTS):
                 slot = slot + jnp.where(rank[k] == i, k, 0)
             perm[t, i] = slot
-            psrc[t, i] = src[row, slot]
+            psrc[t, i] = src[(*row, slot)]
         ends[t, 0] = 0
         for q in range(2 * COLS):
             count = jnp.int32(0)
@@ -94,32 +100,12 @@
                 count = count + (codes[k] <= q).astype(jnp.int32)
             ends[t, q + 1] = count
 
-    @pl.loop(0, SUB)
-    def _(t):
-        sort_level(sub_src, sub_tgt, t, t)
-
-    @pl.loop(0, TOP - 1)
-    def _(t):
-        sort_level(top_src, top_tgt, t, t + SUB)
-
     copies[8].wait()
     copies[4].wait()
     y0 = dot_full(rhs_sub[0], linv[0])
     y_sub[0] = y0
     ylow[r] = y0.astype(BF16)
-    for i in (5, 6, 7, 9, 0, 1, 2, 3):
-        copies[i].wait()
-
-    @pl.loop(0, 6)
-    def _(t):
-        linv_low[t] = linv[t + 1].astype(BF16)
-        uinv_low[t] = uinv[t + 1].astype(BF16)
-
-    @pl.loop(0, COLS)
-    def _(q):
-        pend[q] = jnp.zeros((SIDES, WIDTH), F32)
-
-    pl.semaphore_wait(barrier, 95)
+    pl.semaphore_wait(barrier, 33)
 
     def to(device, src, dst, send_sem, recv_sem):
         copy = pltpu.make_async_remote_copy(
@@ -133,13 +119,29 @@
     other_high = (l ^ 2, r, c)
 
     first = to(other_row, ylow.at[r], ylow_other, misc_send.at[0], misc_recv.at[0])
-    lin_copies = [
-        to(other_row, linv_low.at[t], linv_other.at[t], lin_sem.at[0, t], lin_sem.at[1, t]) for t in range(6)
-    ]
-    rhs_copy = to(
-        other_row, rhs_sub.at[pl.ds(1, SUB - 1)], rhs_sub_other, misc_send.at[1], misc_recv.at[1]
-    )
-    rhs_top_copy = to(other_row, rhs_top.at[pl.ds(0, 2)], rhs_top_other, misc_send.at[2], misc_recv.at[2])
+    copies[10].wait()
+    copies[11].wait()
+    sort_level(sub_src, sub_tgt, (0, 0), 0)
+    for i in (5, 6, 7, 9, 0, 1, 2, 3, 12, 13):
+        copies[i].wait()
+
+    def lin_copy(t):
+        linv_low[t - 1] = linv[t].astype(BF16)
+        return to(other_row, linv_low.at[t - 1], linv_other.at[t - 1], lin_sem.at[0, t - 1], lin_sem.at[1, t - 1])
+
+    def uin_copy(t):
+        uinv_low[t - 1] = uinv[t].astype(BF16)
+        return to(other_row, uinv_low.at[t - 1], uinv_other.at[t - 1], lin_sem.at[2, t - 1], lin_sem.at[3, t - 1])
+
+    def rhs_copy(t):
+        return to(other_row, rhs_sub.at[t], rhs_sub_other.at[t - 1], lin_sem.at[4, t - 1], lin_sem.at[5, t - 1])
+
+    def rhs_top_copy(t):
+        return to(other_row, rhs_top.at[t], rhs_top_other.at[t], lin_sem.at[4, t + 4], lin_sem.at[5, t + 4])
+
+    for t in (1, 2):
+        lin_copy(t)
+        rhs_copy(t)
 
     def wait_linv(t):
         wait_for(linv_other.at[t - 1], lin_sem.at[1, t - 1])
@@ -176,6 +178,7 @@
     def arrive(t):
         wait_for(recv_f.at[t - 1, pl.ds(0, 2 * COLS - 1)], rf_sem.at[t])
         wait_linv(t)
+        wait_for(rhs_sub_other.at[t - 1], lin_sem.at[5, t - 1])
         mine = rhs_sub[t] - add_up(recv_f.at[t - 1, pl.ds(r * COLS, COLS)], SIDES)
         others = rhs_sub_other[t - 1] - add_up(recv_f.at[t - 1, pl.ds((1 - r) * COLS, COLS)], SIDES)
         y = dot_full(mine, linv[t])
@@ -186,13 +189,37 @@
     first.wait_recv()
     first.wait_send()
     ylow[1 - r] = ylow_other[...]
+
+    @pl.loop(0, COLS)
+    def _(q):
+        pend[q] = jnp.zeros((SIDES, WIDTH), F32)
+
     forward(0)
-    rhs_copy.wait_recv()
-
-    @pl.loop(1, SUB - 1)
+    sort_level(sub_src, sub_tgt, (1, 0), 1)
+    arrive(1)
+    for flip in (1, 2):
+        pl.semaphore_signal(group_sem.at[flip - 1], inc=1, device_id=(l ^ flip, r, c), device_id_type=MESH)
+    forward(1)
+    lin_copy(3)
+    rhs_copy(3)
+    sort_level(sub_src, sub_tgt, (2, 0), 2)
+
+    @pl.loop(2, SUB - 1)
     def _(t):
         arrive(t)
         forward(t)
+        lin_copy(t + 2)
+
+        @pl.when(t == 2)
+        def _():
+            rhs_copy(t + 2)
+
+        @pl.when(t == 3)
+        def _():
+            rhs_top_copy(0)
+            rhs_top_copy(1)
+
+        sort_level(sub_src, sub_tgt, (t + 1, 0), t + 1)
 
     t = SUB - 1
     arrive(t)
@@ -210,6 +237,7 @@
     core_out[1] = halves[1, 1 - half].astype(BF16)
     core_copies.append(to(other_core, core_out.at[1], core_in.at[1], misc_send.at[4], misc_recv.at[4]))
     core_copies[0].wait_recv()
+    pl.semaphore_wait(group_sem.at[1], 1)
     slot_5 = high * 2 * COLS + me
     for i in ORDER:
         q = c ^ i
@@ -219,11 +247,14 @@
                 if i or j or flip:
                     to((l ^ flip, r ^ j, q), send_ft.at[0, q], recv_5.at[slot_5], sf_sem.at[t], rf_sem.at[t + 1])
     recv_5[slot_5] = send_ft[0, c]
+    lin_copy(6)
     core_copies[1].wait_recv()
     six[high] = (halves[1, half] + core_in[1].astype(F32)).astype(BF16)
     six_copy = to(other_high, six.at[high], six.at[high], misc_send.at[5], misc_recv.at[5])
-    upper_copy = to(other_row, uinv_low, uinv_other, misc_send.at[6], misc_recv.at[6])
-    rhs_top_copy.wait_recv()
+    for t in (6, 5):
+        uin_copy(t)
+    sort_level(top_src, top_tgt, (0,), SUB)
+    sort_level(top_src, top_tgt, (1,), SUB + 1)
     six_copy.wait_recv()
     for q in range(COLS):
         pend_top[q] = six[0, q].astype(F32) + six[1, q].astype(F32)
@@ -233,6 +264,7 @@
         y_top[t] = y
         if t < TOP - 1:
             wait_linv(t + SUB)
+            wait_for(rhs_top_other.at[t], lin_sem.at[5, t + 4])
             ylow[r, :HALF] = y.astype(BF16)
             ylow[1 - r, :HALF] = dot_split(rhs_top_other[t] - others, linv_other[t + SUB - 1]).astype(BF16)
 
@@ -246,6 +278,8 @@
                 if i or j:
                     to((l, r ^ j, q), send_ft.at[t + 1, q], recv_ft.at[t, me], sf_sem.at[t + SUB], rf_sem.at[t + SUB + 1])
         recv_ft[t, me] = send_ft[t + 1, c]
+        for u in (4 - 2 * t, 3 - 2 * t):
+            uin_copy(u)
         if t == 0:
             for q in range(COLS):
                 pend_top[q] = share(t + SUB, COLS + q, HALF)
@@ -275,7 +309,6 @@
         if i:
             to((l, r, c ^ i), send_bt.at[2, 0], recv_7.at[c], sb_sem.at[7], rb_sem.at[7])
     recv_7[c] = send_bt[2, 0]
-    upper_copy.wait_recv()
     wait_for(recv_7.at[pl.ds(0, COLS - 1)], rb_sem.at[7])
     x_top[pl.ds(COLS, COLS)] = recv_7[...]
 
@@ -283,7 +316,7 @@
         total = None
         for k in range(SLOTS):
             value = dot(load(k), upper[t, k])
-            taken = value * src[row, k].astype(F32)
+            taken = value * src[(*row, k)].astype(F32)
             total = value if total is None else total + value
             second = taken if k == 0 else second + taken
         at_first = r == 0
@@ -292,10 +325,11 @@
 
     def parts_of(t, mine, others, y):
         a = dot_full(y - mine, uinv[t])
+        wait_for(uinv_other.at[t - 1], lin_sem.at[3, t - 1])
         b = -dot_split(others, uinv_other[t - 1])
         return a, b
 
-    mine, others = down(6, lambda k: x_top[COLS + top_tgt[1, k] % COLS], top_src, 1)
+    mine, others = down(6, lambda k: x_top[COLS + top_tgt[1, k] % COLS], top_src, (1,))
     a, b = parts_of(6, mine, others, y_top[1])
     top_mine[1] = a
     send_bt[1, 0] = a.astype(BF16)
@@ -312,11 +346,12 @@
     six_out[...] = x_top[pl.ds(0, COLS)]
     x6_copy = to(other_core, six_out, six_in, misc_send.at[7], misc_recv.at[7])
 
-    mine, others = down(5, lambda k: x_top[top_tgt[0, k]], top_src, 0)
+    mine, others = down(5, lambda k: x_top[top_tgt[0, k]], top_src, (0,))
     a, b = parts_of(5, mine, others, y_top[0])
     top_mine[0] = a
     send_bt[0, 0] = a.astype(BF16)
     send_bt[0, 1] = b.astype(BF16)
+    pl.semaphore_wait(group_sem.at[0], 1)
     slot_a = half * 2 * COLS + c
     for i in ORDER:
         for flip in (1, 0):
@@ -340,9 +375,9 @@
     def down_sub(t):
         return down(
             t,
-            lambda k: x_sub[(t + 1) * COLS + sub_tgt[t, k]].reshape(SIDES, WIDTH),
+            lambda k: x_sub[(t + 1) * COLS + sub_tgt[t, 0, k]].reshape(SIDES, WIDTH),
             sub_src,
-            t,
+            (t, 0),
         )
 
     @pl.loop(0, SUB - 1)
@@ -371,8 +406,12 @@
         top_out[t, half_rows] = top_mine[t]
         top_out[t, pl.ds(pl.multiple_of((1 - half) * HALF, HALF), HALF)] = top_other[t]
 
-    for copy in lin_copies + [rhs_copy, rhs_top_copy, *core_copies, six_copy, upper_copy, x6_copy, top_copy]:
+    for copy in (*core_copies, six_copy, x6_copy, top_copy):
         copy.wait_send()
+    for t in range(6):
+        wait_for(linv_other.at[t], lin_sem.at[0, t])
+        wait_for(uinv_other.at[t], lin_sem.at[2, t])
+        wait_for(rhs_sub_other.at[t] if t < 4 else rhs_top_other.at[t - 4], lin_sem.at[4, t])
     for t in range(SUB - 1):
         wait_for(recv_f.at[t, pl.ds(0, 2 * COLS - 1)], sf_sem.at[t])
     wait_for(recv_5.at[pl.ds(0, 4 * COLS - 1)], sf_sem.at[4])
@@ -388,13 +427,35 @@
     sub_out[0] = dot_full(y_sub[0] - mine - last_in[...], uinv[0])
 
 
+def hand_over(sub, top):
+    def body(sub_in, top_in, sub_res, top_res):
+        sub_res[0, 0, 0] = sub_in[...]
+        top_res[0, 0] = top_in[...]
+
+    vmem_spec = pl.BlockSpec(memory_space=pltpu.VMEM)
+    return pl.pallas_call(
+        body,
+        out_shape=(
+            jax.ShapeDtypeStruct((1, 1, 1) + sub.shape, F32),
+            jax.ShapeDtypeStruct((1, 1) + top.shape, F32),
+        ),
+        in_specs=[vmem_spec] * 2,
+        out_specs=[vmem_spec] * 2,
+    )(sub, top)
+
+
 def local(*args):
     flat = [a.reshape(a.shape[3:] if i < 7 else a.shape[2:]) for i, a in enumerate(args)]
+    flat[5], flat[6] = (a.reshape(SUB, 1, SLOTS) for a in args[5:7])
     vmem, smem, dma = pltpu.VMEM, pltpu.SMEM, pltpu.SemaphoreType.DMA
     tile = (SIDES, WIDTH)
     half = (HALF, WIDTH)
     block = (WIDTH, WIDTH)
     scratch = [
+        smem((SUB, 1, SLOTS), jnp.int32),
+        smem((SUB, 1, SLOTS), jnp.int32),
+        smem((TOP - 1, SLOTS), jnp.int32),
+        smem((TOP - 1, SLOTS), jnp.int32),
         vmem((LINKED, SLOTS) + block, BF16),
         vmem((LINKED, SLOTS) + block, BF16),
         vmem((SUB + TOP,) + block, F32),
@@ -440,8 +501,9 @@
         vmem(tile, F32),
         vmem((TOP,) + half, F32),
         vmem((TOP,) + half, F32),
-        dma((10,)),
-        dma((2, 6)),
+        dma((14,)),
+        dma((6, 6)),
+        pltpu.SemaphoreType.REGULAR((2,)),
         dma((10,)),
         dma((10,)),
         dma((SUB + TOP,)),
@@ -450,7 +512,6 @@
         dma((SUB + TOP,)),
     ]
     any_spec = pl.BlockSpec(memory_space=pl.ANY)
-    smem_spec = pl.BlockSpec(memory_space=pltpu.SMEM)
     vmem_spec = pl.BlockSpec(memory_space=pltpu.VMEM)
     sub, top = pl.pallas_call(
         kernel,
@@ -458,14 +519,14 @@
             jax.ShapeDtypeStruct((SUB,) + tile, F32),
             jax.ShapeDtypeStruct((TOP,) + tile, F32),
         ),
-        in_specs=([any_spec] * 5 + [smem_spec] * 2) * 2,
+        in_specs=[any_spec] * 14,
         out_specs=(vmem_spec, vmem_spec),
         scratch_shapes=scratch,
         compiler_params=pltpu.CompilerParams(
-            collective_id=0, has_side_effects=True, vmem_limit_bytes=40 * 1024 * 1024
+            collective_id=0, has_side_effects=True, vmem_limit_bytes=60 * 1024 * 1024
         ),
     )(*flat)
-    return sub[None, None, None], top[None, None]
+    return hand_over(sub, top)
 
 
 def solution(mesh):

time: 127 us -> 105 us (0.83)
  local copies, waits for them, and re-layouts: 14.7 us -> 0 us
  Pallas kernels: 111 us -> 104 us
    unnamed x27 -> x0, local copies, waits for them, and re-layouts: 14.7 us -> none
    pallas_call x1, Pallas kernels: 111 us -> 103 us  [local(): pl.pallas_call(kernel, out_shape=(jax.ShapeDtypeStruct((SUB,) + tile, F32...]
    pallas_call x0 -> x1, Pallas kernels: none -> 1.54 us  [hand_over(): pl.pallas_call(body, out_shape=(jax.ShapeDtypeStruct((1, 1, 1) + sub.shap...]
where the time goes in v2:
time: 105 us
  Pallas kernels  104 us (99%)
    pallas_call x1, Pallas kernels, local(): pl.pallas_call(kernel, out_shape=(jax.ShapeDtypeStruct((SUB,) + tile, F32...  103 us

profile of v2, /device:TPU:0, one launch (start us, length us, event | category | flops | bytes accessed | tf_op | source)
XLA Modules:
  0.0 104.7 jit_solution(3261865790281585538)
XLA Ops:
  0.6 102.5 %shard_map.149 = (f32[5,32,128]{2,1,0:T(8,128)}, f32[3,32,128]{2,1,0:T(8,128)}) custom-call(f32[5,32,128]{2,1,0:T(8,128)} %bitcast.22, f32[5,128,128]{2,1,0:T(8,128)} %bitcast.18, f32[5,128,128]{2,1,0:T(8,128)} %bitcast.19, bf16[5,16,128,128]{3,2,1,0:T(8,128)(2,1)} %bitcast.14, bf16[5,16,128,128]{3,2,1,0:T(8,128)(2,1)} %bitcast.15, s32[5,1,16]{2,1,0:T(1,128)} %bitcast.24, ...), custom_call_target="tpu_custom_call" | custom-call | tf_op jit(solution)/shard_map/pallas_call | solution.py:516
  103.1 1.5 %shard_map.150 = (f32[1,1,1,5,32,128]{5,4,3,2,1,0:T(8,128)}, f32[1,1,3,32,128]{4,3,2,1,0:T(8,128)}) custom-call(f32[5,32,128]{2,1,0:T(8,128)} %get-tuple-element.4.sub_in, f32[3,32,128]{2,1,0:T(8,128)} %get-tuple-element.5.top_in), custom_call_target="tpu_custom_call" | custom-call | tf_op jit(solution)/shard_map/pallas_call | solution.py:436

commit v3 on v2

v3 whole, which is shorter than its diff:
```python
import jax
import jax.numpy as jnp
from jax import lax
from jax.experimental import pallas as pl
from jax.experimental.pallas import tpu as pltpu
from jax.sharding import PartitionSpec as P

MESH = pl.DeviceIdType.MESH
F32 = jnp.float32
BF16 = jnp.bfloat16
SUB, TOP, SLOTS, COLS, SIDES, WIDTH = 5, 3, 16, 16, 32, 128
HALF = SIDES // 2
LINKED = SUB + TOP - 1
ORDER = (10, 9, 11, 6, 14, 5, 7, 13, 15, 8, 2, 1, 3, 4, 12, 0)


def dot(a, b):
    return jnp.dot(a, b, preferred_element_type=F32)


def dot_full(a, b):
    return jnp.dot(a, b, preferred_element_type=F32, precision=lax.Precision.HIGHEST)


def dot_split(a, b):
    high = a.astype(BF16)
    low = (a - high.astype(F32)).astype(BF16)
    return dot(high, b) + dot(low, b)


def wait_for(ref, sem):
    pltpu.make_async_copy(ref, ref, sem).wait()


def kernel(
    sub_rhs, sub_linv, sub_uinv, sub_lower, sub_upper, sub_src_in, sub_tgt_in,
    top_rhs, top_linv, top_uinv, top_lower, top_upper, top_src_in, top_tgt_in,
    sub_out, top_out,
    sub_src, sub_tgt, top_src, top_tgt,
    lower_0, lower, upper, linv, uinv, rhs_sub, rhs_top,
    linv_low, uinv_low, linv_other, uinv_other, rhs_sub_other, rhs_top_other,
    perm, psrc, ends,
    ylow, ylow_swap, y_sub, y_top, sums, pend, pend_top,
    send_f, recv_f, send_ft, recv_5, recv_ft,
    halves, core_out, core_in, six,
    x_sub, x_top, send_b, recv_b, send_bt, recv_7, recv_6, recv_b5, six_in, six_out, last_out, last_in, top_mine, top_other,
    both_low, load_sem, lin_sem, group_sem, misc_recv, misc_send, rf_sem, sf_sem, rb_sem, sb_sem,
):
    l, r, c = lax.axis_index("layer"), lax.axis_index("prow"), lax.axis_index("pcol")
    high, half = l // 2, l % 2
    half_rows = pl.ds(pl.multiple_of(half * HALF, HALF), HALF)
    me = r * COLS + c

    loads = (
        (sub_lower.at[pl.ds(1, SUB - 1)], lower.at[pl.ds(1, SUB - 1)]),
        (top_lower, lower.at[pl.ds(SUB, TOP - 1)]),
        (sub_upper, upper.at[pl.ds(0, SUB)]),
        (top_upper, upper.at[pl.ds(SUB, TOP - 1)]),
        (sub_linv, linv.at[pl.ds(0, SUB)]),
        (top_linv, linv.at[pl.ds(SUB, TOP)]),
        (sub_uinv, uinv.at[pl.ds(0, SUB)]),
        (top_uinv, uinv.at[pl.ds(SUB, TOP)]),
        (sub_rhs, rhs_sub),
        (top_rhs.at[:, half_rows], rhs_top),
        (sub_src_in, sub_src),
        (sub_tgt_in, sub_tgt),
        (top_src_in, top_src),
        (top_tgt_in, top_tgt),
        (sub_lower.at[0], lower_0),
    )
    copies = [pltpu.make_async_copy(a, b, load_sem.at[i]) for i, (a, b) in enumerate(loads)]
    for i in (8, 4, 10, 11, 14, 9, 5, 12, 13, 6, 7, 0, 1, 2, 3):
        copies[i].start()

    barrier = pltpu.get_barrier_semaphore()
    for flip in (1, 2):
        pl.semaphore_signal(barrier, inc=1, device_id=(l ^ flip, r, c), device_id_type=MESH)
    pl.semaphore_signal(barrier, inc=1, device_id=(l, 1 - r, c), device_id_type=MESH)
    for i in (1, 2, 3, 4, 8, 12):
        pl.semaphore_signal(barrier, inc=1, device_id=(l, r, c ^ i), device_id_type=MESH)

    def sort_level(src, tgt, row, t):
        codes = [tgt[(*row, k)] for k in range(SLOTS)]
        rank = [jnp.int32(0)] * SLOTS
        for k in range(SLOTS):
            for j in range(k):
                before = (codes[j] <= codes[k]).astype(jnp.int32)
                rank[k] = rank[k] + before
                rank[j] = rank[j] + (1 - before)
        for i in range(SLOTS):
            slot = jnp.int32(0)
            for k in range(1, SLOTS):
                slot = slot + jnp.where(rank[k] == i, k, 0)
            perm[t, i] = slot
            psrc[t, i] = src[(*row, slot)]
        ends[t, 0] = 0
        for q in range(2 * COLS):
            count = jnp.int32(0)
            for k in range(SLOTS):
                count = count + (codes[k] <= q).astype(jnp.int32)
            ends[t, q + 1] = count

    copies[8].wait()
    copies[4].wait()
    y0 = dot_full(rhs_sub[0].reshape(SIDES, WIDTH), linv[0]).reshape(2, HALF, WIDTH)
    y_sub[0] = y0
    ylow_swap[0] = y0.astype(BF16)
    for h in range(2):
        ylow[h, r] = ylow_swap[0, h]
    pl.semaphore_wait(barrier, 9)

    def to(device, src, dst, send_sem, recv_sem):
        copy = pltpu.make_async_remote_copy(
            src_ref=src, dst_ref=dst, send_sem=send_sem, recv_sem=recv_sem, device_id=device, device_id_type=MESH
        )
        copy.start()
        return copy

    other_row = (l, 1 - r, c)
    other_core = (l ^ 1, r, c)
    other_high = (l ^ 2, r, c)

    first = to(other_row, ylow_swap.at[0], ylow_swap.at[1], misc_send.at[0], misc_recv.at[0])
    for i in (4, 8, 12):
        pl.semaphore_signal(group_sem.at[2], inc=1, device_id=(l, r, c ^ i), device_id_type=MESH)
    copies[10].wait()
    copies[11].wait()
    sort_level(sub_src, sub_tgt, (0, 0), 0)

    def lin_copy(t):
        linv_low[t - 1] = linv[t].astype(BF16)
        return to(other_row, linv_low.at[t - 1], linv_other.at[t - 1], lin_sem.at[0, t - 1], lin_sem.at[1, t - 1])

    def uin_copy(t):
        uinv_low[t - 1] = uinv[t].astype(BF16)
        return to(other_row, uinv_low.at[t - 1], uinv_other.at[t - 1], lin_sem.at[2, t - 1], lin_sem.at[3, t - 1])

    def rhs_copy(t):
        return to(other_row, rhs_sub.at[t], rhs_sub_other.at[t - 1], lin_sem.at[4, t - 1], lin_sem.at[5, t - 1])

    def rhs_top_copy(t):
        return to(other_row, rhs_top.at[t], rhs_top_other.at[t], lin_sem.at[4, t + 4], lin_sem.at[5, t + 4])

    pl.semaphore_wait(group_sem.at[2], 3)
    pl.semaphore_signal(group_sem.at[3], inc=1, device_id=other_row, device_id_type=MESH)
    for t in (1, 2):
        lin_copy(t)
        rhs_copy(t)
    copies[14].wait()

    def wait_linv(t):
        wait_for(linv_other.at[t - 1], lin_sem.at[1, t - 1])

    streams = (1 - half, half)

    def products(h, t, block):
        total = jnp.zeros((HALF, WIDTH), F32)
        sums[h, 0] = total
        for i in range(SLOTS):
            total = total + dot(ylow[h, psrc[t, i]], block(perm[t, i]))
            sums[h, i + 1] = total

    def share(h, t, code):
        return sums[h, ends[t, code + 1]] - sums[h, ends[t, code]]

    def forward(h, t, block=None):
        products(h, t, block or (lambda k: lower[t, k]))
        for i in ORDER:
            q = c ^ i
            send_f[h, t, q] = (share(h, t, q) + pend[h, q]).astype(BF16)
            for j in (1, 0):
                if i or j:
                    to((l, r ^ j, q), send_f.at[h, t, q], recv_f.at[h, t, me], sf_sem.at[h, t], rf_sem.at[h, t + 1])
        recv_f[h, t, me] = send_f[h, t, c]

    def keep(h, t):
        for q in range(COLS):
            pend[h, q] = share(h, t, COLS + q)

    def add_up(ref, rows):
        parts = [ref[i].astype(F32) for i in range(COLS)]
        while len(parts) > 1:
            parts = [a + b for a, b in zip(parts[::2], parts[1::2])]
        return parts[0]

    def arrive(h, t, first):
        wait_for(recv_f.at[h, t - 1, pl.ds(0, 2 * COLS - 1)], rf_sem.at[h, t])
        if first:
            wait_linv(t)
            wait_for(rhs_sub_other.at[t - 1], lin_sem.at[5, t - 1])
        mine = rhs_sub[t, h] - add_up(recv_f.at[h, t - 1, pl.ds(r * COLS, COLS)], HALF)
        others = rhs_sub_other[t - 1, h] - add_up(recv_f.at[h, t - 1, pl.ds((1 - r) * COLS, COLS)], HALF)
        ylow[h, r] = dot_split(mine, linv_low[t - 1]).astype(BF16)
        ylow[h, 1 - r] = dot_split(others, linv_other[t - 1]).astype(BF16)
        return mine

    def finish(t, mine):
        for h, value in zip(streams, mine):
            keep(h, t)
            y_sub[t, h] = dot_full(value, linv[t])

    def level(t):
        mine = []
        for n, h in enumerate(streams):
            mine.append(arrive(h, t, n == 0))
            forward(h, t)
        finish(t, mine)

    pl.semaphore_wait(group_sem.at[3], 1)
    first.wait_recv()
    first.wait_send()
    for h in range(2):
        ylow[h, 1 - r] = ylow_swap[1, h]

    @pl.loop(0, COLS)
    def _(q):
        for h in range(2):
            pend[h, q] = jnp.zeros((HALF, WIDTH), F32)

    for h in streams:
        forward(h, 0, lambda k: lower_0[k])
    for h in streams:
        keep(h, 0)
    for i in (9, 5, 12, 13, 6, 7, 0, 1, 2, 3):
        copies[i].wait()
    sort_level(sub_src, sub_tgt, (1, 0), 1)
    mine = []
    for n, h in enumerate(streams):
        mine.append(arrive(h, 1, n == 0))
        forward(h, 1)
    finish(1, mine)
    for flip in (1, 2):
        pl.semaphore_signal(group_sem.at[flip - 1], inc=1, device_id=(l ^ flip, r, c), device_id_type=MESH)
    lin_copy(3)
    rhs_copy(3)
    sort_level(sub_src, sub_tgt, (2, 0), 2)

    @pl.loop(2, SUB - 1)
    def _(t):
        level(t)
        lin_copy(t + 2)

        @pl.when(t == 2)
        def _():
            rhs_copy(t + 2)

        @pl.when(t == 3)
        def _():
            rhs_top_copy(0)
            rhs_top_copy(1)

        sort_level(sub_src, sub_tgt, (t + 1, 0), t + 1)

    t = SUB - 1
    theirs = arrive(1 - half, t, True)
    products(1 - half, t, lambda k: lower[t, k])
    for q in range(COLS):
        core_out[0, q] = (share(1 - half, t, q) + pend[1 - half, q]).astype(BF16)
    core_copies = [to(other_core, core_out.at[0], core_in.at[0], misc_send.at[3], misc_recv.at[3])]
    mine = arrive(half, t, False)
    products(half, t, lambda k: lower[t, k])
    for q in range(COLS):
        halves[0, q] = share(half, t, q) + pend[half, q]
    core_copies[0].wait_recv()
    pl.semaphore_wait(group_sem.at[1], 1)
    slot_5 = high * 2 * COLS + me
    for i in ORDER:
        q = c ^ i
        send_ft[0, q] = (halves[0, q] + core_in[0, q].astype(F32)).astype(BF16)
        for flip in (2, 0):
            for j in (1, 0):
                if i or j or flip:
                    to((l ^ flip, r ^ j, q), send_ft.at[0, q], recv_5.at[slot_5], sf_sem.at[0, t], rf_sem.at[0, t + 1])
    recv_5[slot_5] = send_ft[0, c]
    for q in range(COLS):
        core_out[1, q] = share(1 - half, t, COLS + q).astype(BF16)
        halves[1, q] = share(half, t, COLS + q)
    core_copies.append(to(other_core, core_out.at[1], core_in.at[1], misc_send.at[4], misc_recv.at[4]))
    lin_copy(6)
    y_sub[t, 1 - half] = dot_full(theirs, linv[t])
    y_sub[t, half] = dot_full(mine, linv[t])
    core_copies[1].wait_recv()
    six[high] = (halves[1] + core_in[1].astype(F32)).astype(BF16)
    six_copy = to(other_high, six.at[high], six.at[high], misc_send.at[5], misc_recv.at[5])
    for t in (6, 5):
        uin_copy(t)
    sort_level(top_src, top_tgt, (0,), SUB)
    sort_level(top_src, top_tgt, (1,), SUB + 1)
    six_copy.wait_recv()
    for q in range(COLS):
        pend_top[q] = six[0, q].astype(F32) + six[1, q].astype(F32)

    def arrive_top(t, mine, others):
        mine = rhs_top[t] - mine
        if t < TOP - 1:
            wait_linv(t + SUB)
            wait_for(rhs_top_other.at[t], lin_sem.at[5, t + 4])
            ylow[0, r] = dot_split(mine, linv_low[t + SUB - 1]).astype(BF16)
            ylow[0, 1 - r] = dot_split(rhs_top_other[t] - others, linv_other[t + SUB - 1]).astype(BF16)
        return mine

    def forward_top(t):
        products(0, t + SUB, lambda k: lower[t + SUB, k])
        for i in ORDER:
            q = c ^ i
            value = share(0, t + SUB, q) + pend_top[q]
            send_ft[t + 1, q] = value.astype(BF16)
            for j in (1, 0):
                if i or j:
                    to((l, r ^ j, q), send_ft.at[t + 1, q], recv_ft.at[t, me], sf_sem.at[0, t + SUB], rf_sem.at[0, t + SUB + 1])
        recv_ft[t, me] = send_ft[t + 1, c]
        for u in (4 - 2 * t, 3 - 2 * t):
            uin_copy(u)
        if t == 0:
            for q in range(COLS):
                pend_top[q] = share(0, t + SUB, COLS + q)

    wait_for(recv_5.at[pl.ds(0, 4 * COLS - 1)], rf_sem.at[0, SUB])

    def add_up_5(row):
        return add_up(recv_5.at[pl.ds(row * COLS, COLS)], HALF) + add_up(
            recv_5.at[pl.ds((2 + row) * COLS, COLS)], HALF
        )

    value = arrive_top(0, add_up_5(r), add_up_5(1 - r))
    forward_top(0)
    y_top[0] = dot_full(value, linv[SUB])
    for t in (1, 2):
        wait_for(recv_ft.at[t - 1, pl.ds(0, 2 * COLS - 1)], rf_sem.at[0, t + SUB])
        mine = add_up(recv_ft.at[t - 1, pl.ds(r * COLS, COLS)], HALF)
        if t == 1:
            value = arrive_top(1, mine, add_up(recv_ft.at[t - 1, pl.ds((1 - r) * COLS, COLS)], HALF))
            forward_top(1)
            y_top[1] = dot_full(value, linv[SUB + 1])
            both_low[...] = dot_full(linv[7], uinv[7]).astype(BF16)
        else:
            value = arrive_top(2, mine, None)

    send_bt[2, 0] = dot_split(value, both_low[...]).astype(BF16)
    for i in ORDER:
        if i:
            to((l, r, c ^ i), send_bt.at[2, 0], recv_7.at[c], sb_sem.at[0, 7], rb_sem.at[0, 7])
    recv_7[c] = send_bt[2, 0]
    top_mine[2] = dot_full(dot_full(value, linv[7]), uinv[7])
    wait_for(recv_7.at[pl.ds(0, COLS - 1)], rb_sem.at[0, 7])
    x_top[pl.ds(COLS, COLS)] = recv_7[...]

    def down(t, load, src, row):
        total = None
        for k in range(SLOTS):
            value = dot(load(k), upper[t, k])
            taken = value * src[(*row, k)].astype(F32)
            total = value if total is None else total + value
            second = taken if k == 0 else second + taken
        at_first = r == 0
        parts = (total - second, second)
        return jnp.where(at_first, parts[0], parts[1]), jnp.where(at_first, parts[1], parts[0])

    def parts_of(t, mine, others, first=True):
        a = dot_split(mine, uinv_low[t - 1])
        if first:
            wait_for(uinv_other.at[t - 1], lin_sem.at[3, t - 1])
        b = -dot_split(others, uinv_other[t - 1])
        return a, b

    mine, others = down(6, lambda k: x_top[COLS + top_tgt[1, k] % COLS], top_src, (1,))
    mine = y_top[1] - mine
    a, b = parts_of(6, mine, others)
    send_bt[1, 0] = a.astype(BF16)
    send_bt[1, 1] = b.astype(BF16)
    for i in ORDER:
        to((l, 1 - r, c ^ i), send_bt.at[1, 1], recv_6.at[COLS + c], sb_sem.at[0, 6], rb_sem.at[0, 6])
        if i:
            to((l, r, c ^ i), send_bt.at[1, 0], recv_6.at[c], sb_sem.at[0, 6], rb_sem.at[0, 6])
    recv_6[c] = send_bt[1, 0]
    top_mine[1] = dot_full(mine, uinv[6])
    wait_for(recv_6.at[pl.ds(0, 2 * COLS - 1)], rb_sem.at[0, 6])
    for q in range(COLS):
        x_top[q] = (recv_6[q].astype(F32) + recv_6[COLS + q].astype(F32)).astype(BF16)
    top_mine[1] = top_mine[1] + recv_6[COLS + c].astype(F32)
    six_out[...] = x_top[pl.ds(0, COLS)]
    x6_copy = to(other_core, six_out, six_in, misc_send.at[7], misc_recv.at[7])

    mine, others = down(5, lambda k: x_top[top_tgt[0, k]], top_src, (0,))
    mine = y_top[0] - mine
    a, b = parts_of(5, mine, others)
    send_bt[0, 0] = a.astype(BF16)
    send_bt[0, 1] = b.astype(BF16)
    pl.semaphore_wait(group_sem.at[0], 1)
    slot_a = half * 2 * COLS + c
    for i in ORDER:
        for flip in (1, 0):
            to((l ^ flip, 1 - r, c ^ i), send_bt.at[0, 1], recv_b5.at[slot_a + COLS], sb_sem.at[0, 5], rb_sem.at[0, 5])
            if i or flip:
                to((l ^ flip, r, c ^ i), send_bt.at[0, 0], recv_b5.at[slot_a], sb_sem.at[0, 5], rb_sem.at[0, 5])
    recv_b5[slot_a] = send_bt[0, 0]
    top_mine[0] = dot_full(mine, uinv[5])
    x6_copy.wait_recv()
    for q in range(COLS):
        x_sub[half, 6 * COLS + q] = x_top[q]
        x_sub[1 - half, 6 * COLS + q] = six_in[q]
    wait_for(recv_b5.at[pl.ds(0, 4 * COLS - 1)], rb_sem.at[0, 5])
    for q in range(COLS):
        for h in range(2):
            x_sub[h, 5 * COLS + q] = (
                recv_b5[h * 2 * COLS + q].astype(F32) + recv_b5[h * 2 * COLS + COLS + q].astype(F32)
            ).astype(BF16)
    top_mine[0] = top_mine[0] + recv_b5[slot_a + COLS].astype(F32)
    top_copy = to(other_core, top_mine, top_other, misc_send.at[6], misc_recv.at[6])

    def down_sub(h, t):
        return down(t, lambda k: x_sub[h, (t + 1) * COLS + sub_tgt[t, 0, k]], sub_src, (t, 0))

    def climb_down(h, t):
        mine, others = down_sub(h, t)
        mine = y_sub[t, h] - mine
        a, b = parts_of(t, mine, others, h is streams[0])
        send_b[h, t, 0] = a.astype(BF16)
        send_b[h, t, 1] = b.astype(BF16)
        for i in ORDER:
            to((l, 1 - r, c ^ i), send_b.at[h, t, 1], recv_b.at[h, t, COLS + c], sb_sem.at[h, t], rb_sem.at[h, t])
            if i:
                to((l, r, c ^ i), send_b.at[h, t, 0], recv_b.at[h, t, c], sb_sem.at[h, t], rb_sem.at[h, t])
        recv_b[h, t, c] = send_b[h, t, 0]
        return mine

    def solved(h, t):
        wait_for(recv_b.at[h, t, pl.ds(0, 2 * COLS - 1)], rb_sem.at[h, t])
        for q in range(COLS):
            x_sub[h, t * COLS + q] = (recv_b[h, t, q].astype(F32) + recv_b[h, t, COLS + q].astype(F32)).astype(BF16)

    def put_out(h, t, mine):
        rows = pl.ds(pl.multiple_of(h * HALF, HALF), HALF)
        sub_out[t, rows] = dot_full(mine, uinv[t]) + recv_b[h, t, COLS + c].astype(F32)

    kept = [climb_down(h, SUB - 1) for h in streams]

    def descend(step, kept):
        t = SUB - 2 - step
        later = []
        for h in streams:
            solved(h, t + 1)
            later.append(climb_down(h, t))
        for h, value in zip(streams, kept):
            put_out(h, t + 1, value)
        return tuple(later)

    kept = lax.fori_loop(0, SUB - 2, descend, tuple(kept))
    mine, last = [], []
    for n, h in enumerate(streams):
        solved(h, 1)
        value, others = down_sub(h, 0)
        mine.append(value)
        last_out[h] = others
        last.append(to(other_row, last_out.at[h], last_in.at[h], misc_send.at[8 + n], misc_recv.at[8 + n]))
    for h, value in zip(streams, kept):
        put_out(h, 1, value)
    top_copy.wait_recv()
    for t in range(TOP):
        top_out[t, half_rows] = top_mine[t]
        top_out[t, pl.ds(pl.multiple_of((1 - half) * HALF, HALF), HALF)] = top_other[t]

    for copy in (*core_copies, six_copy, x6_copy, top_copy):
        copy.wait_send()
    for t in range(6):
        wait_for(linv_other.at[t], lin_sem.at[0, t])
        wait_for(uinv_other.at[t], lin_sem.at[2, t])
        wait_for(rhs_sub_other.at[t] if t < 4 else rhs_top_other.at[t - 4], lin_sem.at[4, t])
    for t in range(SUB - 1):
        for h in range(2):
            wait_for(recv_f.at[h, t, pl.ds(0, 2 * COLS - 1)], sf_sem.at[h, t])
    wait_for(recv_5.at[pl.ds(0, 4 * COLS - 1)], sf_sem.at[0, 4])
    wait_for(recv_ft.at[0, pl.ds(0, 2 * COLS - 1)], sf_sem.at[0, 5])
    wait_for(recv_ft.at[1, pl.ds(0, 2 * COLS - 1)], sf_sem.at[0, 6])
    wait_for(recv_7.at[pl.ds(0, COLS - 1)], sb_sem.at[0, 7])
    wait_for(recv_6.at[pl.ds(0, 2 * COLS - 1)], sb_sem.at[0, 6])
    wait_for(recv_b5.at[pl.ds(0, 4 * COLS - 1)], sb_sem.at[0, 5])
    for t in range(1, SUB):
        for h in range(2):
            wait_for(recv_b.at[h, t, pl.ds(0, 2 * COLS - 1)], sb_sem.at[h, t])
    for h, value, copy in zip(streams, mine, last):
        copy.wait_send()
        copy.wait_recv()
        rows = pl.ds(pl.multiple_of(h * HALF, HALF), HALF)
        sub_out[0, rows] = dot_full(y_sub[0, h] - value - last_in[h], uinv[0])


def hand_over(sub, top):
    def body(sub_in, top_in, sub_res, top_res):
        sub_res[0, 0, 0] = sub_in[...]
        top_res[0, 0] = top_in[...]

    vmem_spec = pl.BlockSpec(memory_space=pltpu.VMEM)
    return pl.pallas_call(
        body,
        out_shape=(
            jax.ShapeDtypeStruct((1, 1, 1) + sub.shape, F32),
            jax.ShapeDtypeStruct((1, 1) + top.shape, F32),
        ),
        in_specs=[vmem_spec] * 2,
        out_specs=[vmem_spec] * 2,
    )(sub, top)


def local(*args):
    flat = [a.reshape(a.shape[3:] if i < 7 else a.shape[2:]) for i, a in enumerate(args)]
    flat[0] = args[0].reshape(SUB, 2, HALF, WIDTH)
    flat[5], flat[6] = (a.reshape(SUB, 1, SLOTS) for a in args[5:7])
    vmem, smem, dma = pltpu.VMEM, pltpu.SMEM, pltpu.SemaphoreType.DMA
    tile = (SIDES, WIDTH)
    half = (HALF, WIDTH)
    block = (WIDTH, WIDTH)
    scratch = [
        smem((SUB, 1, SLOTS), jnp.int32),
        smem((SUB, 1, SLOTS), jnp.int32),
        smem((TOP - 1, SLOTS), jnp.int32),
        smem((TOP - 1, SLOTS), jnp.int32),
        vmem((SLOTS,) + block, BF16),
        vmem((LINKED, SLOTS) + block, BF16),
        vmem((LINKED, SLOTS) + block, BF16),
        vmem((SUB + TOP,) + block, F32),
        vmem((SUB + TOP,) + block, F32),
        vmem((SUB, 2) + half, F32),
        vmem((TOP,) + half, F32),
        vmem((6,) + block, BF16),
        vmem((6,) + block, BF16),
        vmem((6,) + block, BF16),
        vmem((6,) + block, BF16),
        vmem((SUB - 1, 2) + half, F32),
        vmem((2,) + half, F32),
        smem((LINKED, SLOTS), jnp.int32),
        smem((LINKED, SLOTS), jnp.int32),
        smem((LINKED, 2 * COLS + 1), jnp.int32),
        vmem((2, 2) + half, BF16),
        vmem((2, 2) + half, BF16),
        vmem((SUB, 2) + half, F32),
        vmem((TOP,) + half, F32),
        vmem((2, SLOTS + 1) + half, F32),
        vmem((2, COLS) + half, F32),
        vmem((COLS,) + half, F32),
        vmem((2, SUB - 1, COLS) + half, BF16),
        vmem((2, SUB - 1, 2 * COLS) + half, BF16),
        vmem((TOP, COLS) + half, BF16),
        vmem((4 * COLS,) + half, BF16),
        vmem((2, 2 * COLS) + half, BF16),
        vmem((2, COLS) + half, F32),
        vmem((2, COLS) + half, BF16),
        vmem((2, COLS) + half, BF16),
        vmem((2, COLS) + half, BF16),
        vmem((2, 7 * COLS) + half, BF16),
        vmem((2 * COLS,) + half, BF16),
        vmem((2, SUB, 2) + half, BF16),
        vmem((2, SUB, 2 * COLS) + half, BF16),
        vmem((TOP, 2) + half, BF16),
        vmem((COLS,) + half, BF16),
        vmem((2 * COLS,) + half, BF16),
        vmem((4 * COLS,) + half, BF16),
        vmem((COLS,) + half, BF16),
        vmem((COLS,) + half, BF16),
        vmem((2,) + half, F32),
        vmem((2,) + half, F32),
        vmem((TOP,) + half, F32),
        vmem((TOP,) + half, F32),
        vmem(block, BF16),
        dma((15,)),
        dma((6, 6)),
        pltpu.SemaphoreType.REGULAR((4,)),
        dma((10,)),
        dma((10,)),
        dma((2, SUB + TOP)),
        dma((2, SUB + TOP)),
        dma((2, SUB + TOP)),
        dma((2, SUB + TOP)),
    ]
    any_spec = pl.BlockSpec(memory_space=pl.ANY)
    vmem_spec = pl.BlockSpec(memory_space=pltpu.VMEM)
    sub, top = pl.pallas_call(
        kernel,
        out_shape=(
            jax.ShapeDtypeStruct((SUB,) + tile, F32),
            jax.ShapeDtypeStruct((TOP,) + tile, F32),
        ),
        in_specs=[any_spec] * 14,
        out_specs=(vmem_spec, vmem_spec),
        scratch_shapes=scratch,
        compiler_params=pltpu.CompilerParams(
            collective_id=0, has_side_effects=True, vmem_limit_bytes=60 * 1024 * 1024
        ),
    )(*flat)
    return hand_over(sub, top)


def solution(mesh):
    sub = P("layer", "prow", "pcol")
    top = P("prow", "pcol")
    return jax.shard_map(
        local, mesh=mesh, in_specs=(sub,) * 7 + (top,) * 7, out_specs=(sub, top), check_vma=False
    )
```

time: 105 us -> 101 us (0.962)
  Pallas kernels: 104 us -> 101 us
    pallas_call x1, Pallas kernels: 103 us -> 99 us  [local(): pl.pallas_call(kernel, out_shape=(jax.ShapeDtypeStruct((SUB,) + tile, F32...]
where the time goes in v3:
time: 101 us
  Pallas kernels  101 us (100%)
    pallas_call x1, Pallas kernels, local(): pl.pallas_call(kernel, out_shape=(jax.ShapeDtypeStruct((SUB,) + tile, F32...  99 us

profile of v3, /device:TPU:0, one launch (start us, length us, event | category | flops | bytes accessed | tf_op | source)
XLA Modules:
  0.0 101.2 jit_solution(3708232460345735337)
XLA Ops:
  0.6 99.0 %shard_map.149 = (f32[5,32,128]{2,1,0:T(8,128)}, f32[3,32,128]{2,1,0:T(8,128)}) custom-call(f32[5,2,16,128]{3,2,1,0:T(8,128)} %bitcast.22, f32[5,128,128]{2,1,0:T(8,128)} %bitcast.18, f32[5,128,128]{2,1,0:T(8,128)} %bitcast.19, bf16[5,16,128,128]{3,2,1,0:T(8,128)(2,1)} %bitcast.14, bf16[5,16,128,128]{3,2,1,0:T(8,128)(2,1)} %bitcast.15, ...), custom_call_target="tpu_custom_call" | custom-call | tf_op jit(solution)/shard_map/pallas_call | solution.py:577
  99.7 1.5 %shard_map.150 = (f32[1,1,1,5,32,128]{5,4,3,2,1,0:T(8,128)}, f32[1,1,3,32,128]{4,3,2,1,0:T(8,128)}) custom-call(f32[5,32,128]{2,1,0:T(8,128)} %get-tuple-element.4.sub_in, f32[3,32,128]{2,1,0:T(8,128)} %get-tuple-element.5.top_in), custom_call_target="tpu_custom_call" | custom-call | tf_op jit(solution)/shard_map/pallas_call | solution.py:494

commit v4 on v3

--- a/solution.py
+++ b/solution.py
@@ -38,9 +38,9 @@
     sub_out, top_out,
     sub_src, sub_tgt, top_src, top_tgt,
     lower_0, lower, upper, linv, uinv, rhs_sub, rhs_top,
-    linv_low, uinv_low, linv_other, uinv_other, rhs_sub_other, rhs_top_other,
+    linv_low, uinv_low, linv_other, uinv_other, pair, rhs_sub_other, rhs_top_other,
     perm, psrc, ends,
-    ylow, ylow_swap, y_sub, y_top, sums, pend, pend_top,
+    ylow, ylow_swap, yu_sub, yu_top, sums, pend, pend_top,
     send_f, recv_f, send_ft, recv_5, recv_ft,
     halves, core_out, core_in, six,
     x_sub, x_top, send_b, recv_b, send_bt, recv_7, recv_6, recv_b5, six_in, six_out, last_out, last_in, top_mine, top_other,
@@ -69,7 +69,7 @@
         (sub_lower.at[0], lower_0),
     )
     copies = [pltpu.make_async_copy(a, b, load_sem.at[i]) for i, (a, b) in enumerate(loads)]
-    for i in (8, 4, 10, 11, 14, 9, 5, 12, 13, 6, 7, 0, 1, 2, 3):
+    for i in (8, 4, 10, 11, 14, 9, 5, 12, 13, 0, 1):
         copies[i].start()
 
     barrier = pltpu.get_barrier_semaphore()
@@ -103,7 +103,6 @@
     copies[8].wait()
     copies[4].wait()
     y0 = dot_full(rhs_sub[0].reshape(SIDES, WIDTH), linv[0]).reshape(2, HALF, WIDTH)
-    y_sub[0] = y0
     ylow_swap[0] = y0.astype(BF16)
     for h in range(2):
         ylow[h, r] = ylow_swap[0, h]
@@ -132,8 +131,8 @@
         return to(other_row, linv_low.at[t - 1], linv_other.at[t - 1], lin_sem.at[0, t - 1], lin_sem.at[1, t - 1])
 
     def uin_copy(t):
-        uinv_low[t - 1] = uinv[t].astype(BF16)
-        return to(other_row, uinv_low.at[t - 1], uinv_other.at[t - 1], lin_sem.at[2, t - 1], lin_sem.at[3, t - 1])
+        uinv_low[t] = uinv[t].astype(BF16)
+        return to(other_row, uinv_low.at[t], uinv_other.at[t], lin_sem.at[2, t], lin_sem.at[3, t])
 
     def rhs_copy(t):
         return to(other_row, rhs_sub.at[t], rhs_sub_other.at[t - 1], lin_sem.at[4, t - 1], lin_sem.at[5, t - 1])
@@ -143,13 +142,26 @@
 
     pl.semaphore_wait(group_sem.at[2], 3)
     pl.semaphore_signal(group_sem.at[3], inc=1, device_id=other_row, device_id_type=MESH)
-    for t in (1, 2):
-        lin_copy(t)
-        rhs_copy(t)
+    lin_copy(1)
+    rhs_copy(1)
     copies[14].wait()
 
-    def wait_linv(t):
+    def prepare_lower(t, src, row):
         wait_for(linv_other.at[t - 1], lin_sem.at[1, t - 1])
+        pair[r] = linv_low[t - 1]
+        pair[1 - r] = linv_other[t - 1]
+        for k in range(SLOTS):
+            lower[t, k] = dot(pair[src[(*row, k)]], lower[t, k]).astype(BF16)
+
+    def prepare_upper(t, src, row):
+        wait_for(uinv_other.at[t], lin_sem.at[3, t])
+        pair[r] = uinv_low[t]
+        pair[1 - r] = uinv_other[t]
+        for k in range(SLOTS):
+            upper[t, k] = dot(upper[t, k], pair[src[(*row, k)]]).astype(BF16)
+
+    def solve_both(value, t):
+        return dot_full(dot_full(value, linv[t]), uinv[t])
 
     streams = (1 - half, half)
 
@@ -186,18 +198,17 @@
     def arrive(h, t, first):
         wait_for(recv_f.at[h, t - 1, pl.ds(0, 2 * COLS - 1)], rf_sem.at[h, t])
         if first:
-            wait_linv(t)
             wait_for(rhs_sub_other.at[t - 1], lin_sem.at[5, t - 1])
         mine = rhs_sub[t, h] - add_up(recv_f.at[h, t - 1, pl.ds(r * COLS, COLS)], HALF)
         others = rhs_sub_other[t - 1, h] - add_up(recv_f.at[h, t - 1, pl.ds((1 - r) * COLS, COLS)], HALF)
-        ylow[h, r] = dot_split(mine, linv_low[t - 1]).astype(BF16)
-        ylow[h, 1 - r] = dot_split(others, linv_other[t - 1]).astype(BF16)
+        ylow[h, r] = mine.astype(BF16)
+        ylow[h, 1 - r] = others.astype(BF16)
         return mine
 
     def finish(t, mine):
         for h, value in zip(streams, mine):
             keep(h, t)
-            y_sub[t, h] = dot_full(value, linv[t])
+            yu_sub[t, h] = solve_both(value, t)
 
     def level(t):
         mine = []
@@ -219,11 +230,19 @@
 
     for h in streams:
         forward(h, 0, lambda k: lower_0[k])
+    for i in (6, 7, 2, 3):
+        copies[i].start()
     for h in streams:
         keep(h, 0)
-    for i in (9, 5, 12, 13, 6, 7, 0, 1, 2, 3):
+    for i in (9, 5, 12, 13, 0, 1):
         copies[i].wait()
+    lin_copy(2)
+    rhs_copy(2)
     sort_level(sub_src, sub_tgt, (1, 0), 1)
+    prepare_lower(1, sub_src, (1, 0))
+    for i in (6, 7, 2, 3):
+        copies[i].wait()
+    yu_sub[0] = dot_full(y0.reshape(SIDES, WIDTH), uinv[0]).reshape(2, HALF, WIDTH)
     mine = []
     for n, h in enumerate(streams):
         mine.append(arrive(h, 1, n == 0))
@@ -234,6 +253,7 @@
     lin_copy(3)
     rhs_copy(3)
     sort_level(sub_src, sub_tgt, (2, 0), 2)
+    prepare_lower(2, sub_src, (2, 0))
 
     @pl.loop(2, SUB - 1)
     def _(t):
@@ -250,6 +270,7 @@
             rhs_top_copy(1)
 
         sort_level(sub_src, sub_tgt, (t + 1, 0), t + 1)
+        prepare_lower(t + 1, sub_src, (t + 1, 0))
 
     t = SUB - 1
     theirs = arrive(1 - half, t, True)
@@ -277,15 +298,14 @@
         halves[1, q] = share(half, t, COLS + q)
     core_copies.append(to(other_core, core_out.at[1], core_in.at[1], misc_send.at[4], misc_recv.at[4]))
     lin_copy(6)
-    y_sub[t, 1 - half] = dot_full(theirs, linv[t])
-    y_sub[t, half] = dot_full(mine, linv[t])
+    yu_sub[t, 1 - half] = solve_both(theirs, t)
+    yu_sub[t, half] = solve_both(mine, t)
     core_copies[1].wait_recv()
     six[high] = (halves[1] + core_in[1].astype(F32)).astype(BF16)
     six_copy = to(other_high, six.at[high], six.at[high], misc_send.at[5], misc_recv.at[5])
-    for t in (6, 5):
-        uin_copy(t)
     sort_level(top_src, top_tgt, (0,), SUB)
     sort_level(top_src, top_tgt, (1,), SUB + 1)
+    prepare_lower(SUB, top_src, (0,))
     six_copy.wait_recv()
     for q in range(COLS):
         pend_top[q] = six[0, q].astype(F32) + six[1, q].astype(F32)
@@ -293,10 +313,9 @@
     def arrive_top(t, mine, others):
         mine = rhs_top[t] - mine
         if t < TOP - 1:
-            wait_linv(t + SUB)
             wait_for(rhs_top_other.at[t], lin_sem.at[5, t + 4])
-            ylow[0, r] = dot_split(mine, linv_low[t + SUB - 1]).astype(BF16)
-            ylow[0, 1 - r] = dot_split(rhs_top_other[t] - others, linv_other[t + SUB - 1]).astype(BF16)
+            ylow[0, r] = mine.astype(BF16)
+            ylow[0, 1 - r] = (rhs_top_other[t] - others).astype(BF16)
         return mine
 
     def forward_top(t):
@@ -305,15 +324,17 @@
             q = c ^ i
             value = share(0, t + SUB, q) + pend_top[q]
             send_ft[t + 1, q] = value.astype(BF16)
-            for j in (1, 0):
+            for j in (1, 0) if t == 0 else (0,):
                 if i or j:
-                    to((l, r ^ j, q), send_ft.at[t + 1, q], recv_ft.at[t, me], sf_sem.at[0, t + SUB], rf_sem.at[0, t + SUB + 1])
-        recv_ft[t, me] = send_ft[t + 1, c]
-        for u in (4 - 2 * t, 3 - 2 * t):
-            uin_copy(u)
+                    to((l, r ^ j, q), send_ft.at[t + 1, q], recv_ft.at[t, me if t == 0 else c], sf_sem.at[0, t + SUB], rf_sem.at[0, t + SUB + 1])
+        recv_ft[t, me if t == 0 else c] = send_ft[t + 1, c]
         if t == 0:
             for q in range(COLS):
                 pend_top[q] = share(0, t + SUB, COLS + q)
+            uin_copy(6)
+        else:
+            for u in (5, 4, 3):
+                uin_copy(u)
 
     wait_for(recv_5.at[pl.ds(0, 4 * COLS - 1)], rf_sem.at[0, SUB])
 
@@ -324,14 +345,15 @@
 
     value = arrive_top(0, add_up_5(r), add_up_5(1 - r))
     forward_top(0)
-    y_top[0] = dot_full(value, linv[SUB])
+    prepare_lower(SUB + 1, top_src, (1,))
+    yu_top[0] = solve_both(value, SUB)
     for t in (1, 2):
-        wait_for(recv_ft.at[t - 1, pl.ds(0, 2 * COLS - 1)], rf_sem.at[0, t + SUB])
-        mine = add_up(recv_ft.at[t - 1, pl.ds(r * COLS, COLS)], HALF)
+        wait_for(recv_ft.at[t - 1, pl.ds(0, (2 * COLS if t == 1 else COLS) - 1)], rf_sem.at[0, t + SUB])
+        mine = add_up(recv_ft.at[t - 1, pl.ds(r * COLS if t == 1 else 0, COLS)], HALF)
         if t == 1:
             value = arrive_top(1, mine, add_up(recv_ft.at[t - 1, pl.ds((1 - r) * COLS, COLS)], HALF))
             forward_top(1)
-            y_top[1] = dot_full(value, linv[SUB + 1])
+            yu_top[1] = solve_both(value, SUB + 1)
             both_low[...] = dot_full(linv[7], uinv[7]).astype(BF16)
         else:
             value = arrive_top(2, mine, None)
@@ -342,6 +364,9 @@
             to((l, r, c ^ i), send_bt.at[2, 0], recv_7.at[c], sb_sem.at[0, 7], rb_sem.at[0, 7])
     recv_7[c] = send_bt[2, 0]
     top_mine[2] = dot_full(dot_full(value, linv[7]), uinv[7])
+    for u in (2, 1, 0):
+        uin_copy(u)
+    prepare_upper(6, top_src, (1,))
     wait_for(recv_7.at[pl.ds(0, COLS - 1)], rb_sem.at[0, 7])
     x_top[pl.ds(COLS, COLS)] = recv_7[...]
 
@@ -356,16 +381,8 @@
         parts = (total - second, second)
         return jnp.where(at_first, parts[0], parts[1]), jnp.where(at_first, parts[1], parts[0])
 
-    def parts_of(t, mine, others, first=True):
-        a = dot_split(mine, uinv_low[t - 1])
-        if first:
-            wait_for(uinv_other.at[t - 1], lin_sem.at[3, t - 1])
-        b = -dot_split(others, uinv_other[t - 1])
-        return a, b
-
     mine, others = down(6, lambda k: x_top[COLS + top_tgt[1, k] % COLS], top_src, (1,))
-    mine = y_top[1] - mine
-    a, b = parts_of(6, mine, others)
+    a, b = yu_top[1] - mine, -others
     send_bt[1, 0] = a.astype(BF16)
     send_bt[1, 1] = b.astype(BF16)
     for i in ORDER:
@@ -373,7 +390,8 @@
         if i:
             to((l, r, c ^ i), send_bt.at[1, 0], recv_6.at[c], sb_sem.at[0, 6], rb_sem.at[0, 6])
     recv_6[c] = send_bt[1, 0]
-    top_mine[1] = dot_full(mine, uinv[6])
+    top_mine[1] = a
+    prepare_upper(5, top_src, (0,))
     wait_for(recv_6.at[pl.ds(0, 2 * COLS - 1)], rb_sem.at[0, 6])
     for q in range(COLS):
         x_top[q] = (recv_6[q].astype(F32) + recv_6[COLS + q].astype(F32)).astype(BF16)
@@ -382,8 +400,7 @@
     x6_copy = to(other_core, six_out, six_in, misc_send.at[7], misc_recv.at[7])
 
     mine, others = down(5, lambda k: x_top[top_tgt[0, k]], top_src, (0,))
-    mine = y_top[0] - mine
-    a, b = parts_of(5, mine, others)
+    a, b = yu_top[0] - mine, -others
     send_bt[0, 0] = a.astype(BF16)
     send_bt[0, 1] = b.astype(BF16)
     pl.semaphore_wait(group_sem.at[0], 1)
@@ -394,7 +411,8 @@
             if i or flip:
                 to((l ^ flip, r, c ^ i), send_bt.at[0, 0], recv_b5.at[slot_a], sb_sem.at[0, 5], rb_sem.at[0, 5])
     recv_b5[slot_a] = send_bt[0, 0]
-    top_mine[0] = dot_full(mine, uinv[5])
+    top_mine[0] = a
+    prepare_upper(4, sub_src, (4, 0))
     x6_copy.wait_recv()
     for q in range(COLS):
         x_sub[half, 6 * COLS + q] = x_top[q]
@@ -413,8 +431,7 @@
 
     def climb_down(h, t):
         mine, others = down_sub(h, t)
-        mine = y_sub[t, h] - mine
-        a, b = parts_of(t, mine, others, h is streams[0])
+        a, b = yu_sub[t, h] - mine, -others
         send_b[h, t, 0] = a.astype(BF16)
         send_b[h, t, 1] = b.astype(BF16)
         for i in ORDER:
@@ -422,7 +439,7 @@
             if i:
                 to((l, r, c ^ i), send_b.at[h, t, 0], recv_b.at[h, t, c], sb_sem.at[h, t], rb_sem.at[h, t])
         recv_b[h, t, c] = send_b[h, t, 0]
-        return mine
+        return a
 
     def solved(h, t):
         wait_for(recv_b.at[h, t, pl.ds(0, 2 * COLS - 1)], rb_sem.at[h, t])
@@ -431,9 +448,10 @@
 
     def put_out(h, t, mine):
         rows = pl.ds(pl.multiple_of(h * HALF, HALF), HALF)
-        sub_out[t, rows] = dot_full(mine, uinv[t]) + recv_b[h, t, COLS + c].astype(F32)
+        sub_out[t, rows] = mine + recv_b[h, t, COLS + c].astype(F32)
 
     kept = [climb_down(h, SUB - 1) for h in streams]
+    prepare_upper(SUB - 2, sub_src, (SUB - 2, 0))
 
     def descend(step, kept):
         t = SUB - 2 - step
@@ -443,6 +461,7 @@
             later.append(climb_down(h, t))
         for h, value in zip(streams, kept):
             put_out(h, t + 1, value)
+        prepare_upper(t - 1, sub_src, (t - 1, 0))
         return tuple(later)
 
     kept = lax.fori_loop(0, SUB - 2, descend, tuple(kept))
@@ -450,8 +469,8 @@
     for n, h in enumerate(streams):
         solved(h, 1)
         value, others = down_sub(h, 0)
-        mine.append(value)
-        last_out[h] = others
+        mine.append(yu_sub[0, h] - value)
+        last_out[h] = -others
         last.append(to(other_row, last_out.at[h], last_in.at[h], misc_send.at[8 + n], misc_recv.at[8 + n]))
     for h, value in zip(streams, kept):
         put_out(h, 1, value)
@@ -462,16 +481,17 @@
 
     for copy in (*core_copies, six_copy, x6_copy, top_copy):
         copy.wait_send()
+    for t in range(LINKED):
+        wait_for(uinv_other.at[t], lin_sem.at[2, t])
     for t in range(6):
         wait_for(linv_other.at[t], lin_sem.at[0, t])
-        wait_for(uinv_other.at[t], lin_sem.at[2, t])
         wait_for(rhs_sub_other.at[t] if t < 4 else rhs_top_other.at[t - 4], lin_sem.at[4, t])
     for t in range(SUB - 1):
         for h in range(2):
             wait_for(recv_f.at[h, t, pl.ds(0, 2 * COLS - 1)], sf_sem.at[h, t])
     wait_for(recv_5.at[pl.ds(0, 4 * COLS - 1)], sf_sem.at[0, 4])
     wait_for(recv_ft.at[0, pl.ds(0, 2 * COLS - 1)], sf_sem.at[0, 5])
-    wait_for(recv_ft.at[1, pl.ds(0, 2 * COLS - 1)], sf_sem.at[0, 6])
+    wait_for(recv_ft.at[1, pl.ds(0, COLS - 1)], sf_sem.at[0, 6])
     wait_for(recv_7.at[pl.ds(0, COLS - 1)], sb_sem.at[0, 7])
     wait_for(recv_6.at[pl.ds(0, 2 * COLS - 1)], sb_sem.at[0, 6])
     wait_for(recv_b5.at[pl.ds(0, 4 * COLS - 1)], sb_sem.at[0, 5])
@@ -482,7 +502,7 @@
         copy.wait_send()
         copy.wait_recv()
         rows = pl.ds(pl.multiple_of(h * HALF, HALF), HALF)
-        sub_out[0, rows] = dot_full(y_sub[0, h] - value - last_in[h], uinv[0])
+        sub_out[0, rows] = value + last_in[h]
 
 
 def hand_over(sub, top):
@@ -523,9 +543,10 @@
         vmem((SUB, 2) + half, F32),
         vmem((TOP,) + half, F32),
         vmem((6,) + block, BF16),
+        vmem((LINKED,) + block, BF16),
         vmem((6,) + block, BF16),
-        vmem((6,) + block, BF16),
-        vmem((6,) + block, BF16),
+        vmem((LINKED,) + block, BF16),
+        vmem((2,) + block, BF16),
         vmem((SUB - 1, 2) + half, F32),
         vmem((2,) + half, F32),
         smem((LINKED, SLOTS), jnp.int32),
@@ -563,7 +584,7 @@
         vmem((TOP,) + half, F32),
         vmem(block, BF16),
         dma((15,)),
-        dma((6, 6)),
+        dma((6, LINKED)),
         pltpu.SemaphoreType.REGULAR((4,)),
         dma((10,)),
         dma((10,)),

time: 101 us -> 97.3 us (0.963)
  Pallas kernels: 101 us -> 96.5 us
    pallas_call x1, Pallas kernels: 99 us -> 94.9 us  [local(): pl.pallas_call(kernel, out_shape=(jax.ShapeDtypeStruct((SUB,) + tile, F32...]
where the time goes in v4:
time: 97.3 us; the launch traced here: 97.1 us
  Pallas kernels  96.5 us (99%)
    pallas_call x1, Pallas kernels, local(): pl.pallas_call(kernel, out_shape=(jax.ShapeDtypeStruct((SUB,) + tile, F32...  94.9 us

profile of v4, /device:TPU:0, one launch (start us, length us, event | category | flops | bytes accessed | tf_op | source)
XLA Modules:
  0.0 97.1 jit_solution(16991552674170981378)
XLA Ops:
  0.6 94.9 %shard_map.149 = (f32[5,32,128]{2,1,0:T(8,128)}, f32[3,32,128]{2,1,0:T(8,128)}) custom-call(f32[5,2,16,128]{3,2,1,0:T(8,128)} %bitcast.22, f32[5,128,128]{2,1,0:T(8,128)} %bitcast.18, f32[5,128,128]{2,1,0:T(8,128)} %bitcast.19, bf16[5,16,128,128]{3,2,1,0:T(8,128)(2,1)} %bitcast.14, bf16[5,16,128,128]{3,2,1,0:T(8,128)(2,1)} %bitcast.15, ...), custom_call_target="tpu_custom_call" | custom-call | tf_op jit(solution)/shard_map/pallas_call | solution.py:598
  95.6 1.5 %shard_map.150 = (f32[1,1,1,5,32,128]{5,4,3,2,1,0:T(8,128)}, f32[1,1,3,32,128]{4,3,2,1,0:T(8,128)}) custom-call(f32[5,32,128]{2,1,0:T(8,128)} %get-tuple-element.4.sub_in, f32[3,32,128]{2,1,0:T(8,128)} %get-tuple-element.5.top_in), custom_call_target="tpu_custom_call" | custom-call | tf_op jit(solution)/shard_map/pallas_call | solution.py:514

commit v5 on v4

--- a/solution.py
+++ b/solution.py
@@ -506,26 +506,34 @@
 
 
 def hand_over(sub, top):
-    def body(sub_in, top_in, sub_res, top_res):
-        sub_res[0, 0, 0] = sub_in[...]
-        top_res[0, 0] = top_in[...]
-
-    vmem_spec = pl.BlockSpec(memory_space=pltpu.VMEM)
+    def body(sub_in, top_in, sub_res, top_res, sems):
+        copies = [
+            pltpu.make_async_copy(sub_in, sub_res.at[0, 0, 0], sems.at[0]),
+            pltpu.make_async_copy(top_in, top_res.at[0, 0], sems.at[1]),
+        ]
+        for copy in copies:
+            copy.start()
+        for copy in copies:
+            copy.wait()
+
+    any_spec = pl.BlockSpec(memory_space=pl.ANY)
     return pl.pallas_call(
         body,
         out_shape=(
             jax.ShapeDtypeStruct((1, 1, 1) + sub.shape, F32),
             jax.ShapeDtypeStruct((1, 1) + top.shape, F32),
         ),
-        in_specs=[vmem_spec] * 2,
-        out_specs=[vmem_spec] * 2,
-    )(sub, top)
+        in_specs=[any_spec] * 2,
+        out_specs=[any_spec] * 2,
+        scratch_shapes=[pltpu.SemaphoreType.DMA((2,))],
+    )(pltpu.with_memory_space_constraint(sub, pltpu.VMEM), pltpu.with_memory_space_constraint(top, pltpu.VMEM))
 
 
 def local(*args):
     flat = [a.reshape(a.shape[3:] if i < 7 else a.shape[2:]) for i, a in enumerate(args)]
     flat[0] = args[0].reshape(SUB, 2, HALF, WIDTH)
     flat[5], flat[6] = (a.reshape(SUB, 1, SLOTS) for a in args[5:7])
+    flat = [pltpu.with_memory_space_constraint(a, pltpu.HBM) for a in flat]
     vmem, smem, dma = pltpu.VMEM, pltpu.SMEM, pltpu.SemaphoreType.DMA
     tile = (SIDES, WIDTH)
     half = (HALF, WIDTH)
@@ -605,7 +613,7 @@
         out_specs=(vmem_spec, vmem_spec),
         scratch_shapes=scratch,
         compiler_params=pltpu.CompilerParams(
-            collective_id=0, has_side_effects=True, vmem_limit_bytes=60 * 1024 * 1024
+            collective_id=0, has_side_effects=True, vmem_limit_bytes=48 * 1024 * 1024
         ),
     )(*flat)
     return hand_over(sub, top)

time: 97.3 us -> 95.9 us (0.986)
  Pallas kernels: 96.5 us -> 95 us
where the time goes in v5:
time: 95.9 us; the launch traced here: 95.8 us
  Pallas kernels  95 us (99%)
    pallas_call x1, Pallas kernels, local(): pl.pallas_call(kernel, out_shape=(jax.ShapeDtypeStruct((SUB,) + tile, F32...  94.3 us

profile of v5, /device:TPU:0, one launch (start us, length us, event | category | flops | bytes accessed | tf_op | source)
XLA Modules:
  0.0 95.8 jit_solution(10408766893798989428)
XLA Ops:
  0.6 94.3 %shard_map.149 = (f32[5,32,128]{2,1,0:T(8,128)S(1)}, f32[3,32,128]{2,1,0:T(8,128)S(1)}) custom-call(f32[5,2,16,128]{3,2,1,0:T(8,128)} %bitcast.22, f32[5,128,128]{2,1,0:T(8,128)} %bitcast.18, f32[5,128,128]{2,1,0:T(8,128)} %bitcast.19, bf16[5,16,128,128]{3,2,1,0:T(8,128)(2,1)} %bitcast.14, bf16[5,16,128,128]{3,2,1,0:T(8,128)(2,1)} %bitcast.15, ...), custom_call_target="tpu_custom_call" | custom-call | tf_op jit(solution)/shard_map/pallas_call | solution.py:606
  95.0 0.7 shard_map.150

commit v6 on v5

--- a/solution.py
+++ b/solution.py
@@ -11,7 +11,7 @@
 SUB, TOP, SLOTS, COLS, SIDES, WIDTH = 5, 3, 16, 16, 32, 128
 HALF = SIDES // 2
 LINKED = SUB + TOP - 1
-ORDER = (10, 9, 11, 6, 14, 5, 7, 13, 15, 8, 2, 1, 3, 4, 12, 0)
+ORDER = (10, 11, 14, 9, 6, 15, 7, 13, 5, 8, 2, 3, 12, 1, 4, 0)
 
 
 def dot(a, b):
@@ -210,11 +210,25 @@
             keep(h, t)
             yu_sub[t, h] = solve_both(value, t)
 
+    def early(t):
+        lin_copy(t + 2)
+
+        @pl.when(t == 2)
+        def _():
+            rhs_copy(t + 2)
+
+        @pl.when(t == 3)
+        def _():
+            rhs_top_copy(0)
+            rhs_top_copy(1)
+
     def level(t):
         mine = []
         for n, h in enumerate(streams):
             mine.append(arrive(h, t, n == 0))
             forward(h, t)
+            if n == 0:
+                early(t)
         finish(t, mine)
 
     pl.semaphore_wait(group_sem.at[3], 1)
@@ -247,28 +261,18 @@
     for n, h in enumerate(streams):
         mine.append(arrive(h, 1, n == 0))
         forward(h, 1)
+        if n == 0:
+            lin_copy(3)
+            rhs_copy(3)
     finish(1, mine)
     for flip in (1, 2):
         pl.semaphore_signal(group_sem.at[flip - 1], inc=1, device_id=(l ^ flip, r, c), device_id_type=MESH)
-    lin_copy(3)
-    rhs_copy(3)
     sort_level(sub_src, sub_tgt, (2, 0), 2)
     prepare_lower(2, sub_src, (2, 0))
 
     @pl.loop(2, SUB - 1)
     def _(t):
         level(t)
-        lin_copy(t + 2)
-
-        @pl.when(t == 2)
-        def _():
-            rhs_copy(t + 2)
-
-        @pl.when(t == 3)
-        def _():
-            rhs_top_copy(0)
-            rhs_top_copy(1)
-
         sort_level(sub_src, sub_tgt, (t + 1, 0), t + 1)
         prepare_lower(t + 1, sub_src, (t + 1, 0))
 

time: 95.9 us -> 95.3 us (level)
  no operation moved by 1% of the time
where the time goes in v6:
time: 95.3 us; the launch traced here: 95.2 us
  Pallas kernels  94.4 us (99%)
    pallas_call x1, Pallas kernels, local(): pl.pallas_call(kernel, out_shape=(jax.ShapeDtypeStruct((SUB,) + tile, F32...  93.7 us

profile of v6, /device:TPU:0, one launch (start us, length us, event | category | flops | bytes accessed | tf_op | source)
XLA Modules:
  0.0 95.2 jit_solution(1443488553963134849)
XLA Ops:
  0.6 93.7 %shard_map.149 = (f32[5,32,128]{2,1,0:T(8,128)S(1)}, f32[3,32,128]{2,1,0:T(8,128)S(1)}) custom-call(f32[5,2,16,128]{3,2,1,0:T(8,128)} %bitcast.22, f32[5,128,128]{2,1,0:T(8,128)} %bitcast.18, f32[5,128,128]{2,1,0:T(8,128)} %bitcast.19, bf16[5,16,128,128]{3,2,1,0:T(8,128)(2,1)} %bitcast.14, bf16[5,16,128,128]{3,2,1,0:T(8,128)(2,1)} %bitcast.15, ...), custom_call_target="tpu_custom_call" | custom-call | tf_op jit(solution)/shard_map/pallas_call | solution.py:610
  94.4 0.7 shard_map.150
